TPU v7x, 32 devices: a whole 2x2x4 slice. The times are simulated.
32 devices in a mesh: dp: 4 (over x, core), fsdp: 4 (over z), ctx: 2 (over y).
Axes of the slice: x: 2, y: 2, z: 4, core: 2. Of those that a mesh axis runs over, the one named last changes fastest.
Arguments:
- tokens: bfloat16 [16, 768, 1024], P(('dp', 'fsdp'), 'ctx'), may hold values from -24 to 24
- w_query: bfloat16 [1024, 1024], P(('fsdp', 'ctx'))
- w_key: bfloat16 [1024, 1024], P(('fsdp', 'ctx'))
- w_value: bfloat16 [1024, 1024], P(('fsdp', 'ctx')), may hold values from -0.1875 to 0.1875
- w_output: bfloat16 [1024, 1024], P(('fsdp', 'ctx')), may hold values from -0.1875 to 0.1875
- grad_out: bfloat16 [16, 768, 1024], P(('dp', 'fsdp'), 'ctx'), may hold values from -6 to 6
- doc_lengths: int32 [16, 8], P(('dp', 'fsdp')), may hold values from 1 to 384, 768 in all within a row
- block_ids: int32 [16, 6, 8], replicated, may hold values from 0 to 5, as said below
Outputs:
- layer_out: bfloat16 [16, 768, 1024], P(('dp', 'fsdp'), 'ctx')
- grad_tokens: bfloat16 [16, 768, 1024], P(('dp', 'fsdp'), 'ctx')
- grad_w_query: float32 [1024, 1024], P(('fsdp', 'ctx'))
- grad_w_key: float32 [1024, 1024], P(('fsdp', 'ctx'))
- grad_w_value: float32 [1024, 1024], P(('fsdp', 'ctx'))
- grad_w_output: float32 [1024, 1024], P(('fsdp', 'ctx'))
Inputs may be any that keep to these rules, and one draw needn't show every extreme that they name: `doc_lengths`: each row holds 8 lengths that sum to 768; the largest is exactly 384. `block_ids`: for head h and query block j, entries 0, 1, 2 are j - 1, j, j + 1 modulo 6, entry 3 is 0, and the other 4 entries are drawn at random; entries may repeat.
All inputs are finite; a program needn't handle non-finite values.
Results may differ from a plain program's by a relative error of at most 0.039.
Values may be sent and summed in bfloat16 or wider, within the bound.
A program may use at most 128 MiB of HBM per device.

v0:
```python
import math

import jax
import jax.numpy as jnp
from jax import lax
from jax.sharding import PartitionSpec as P

HEADS = 16
HEAD_DIM = 64
BLOCK = 128


def contract_last(left_rows, right_rows):
    return lax.dot_general(
        left_rows, right_rows, (((1,), (1,)), ((), ())), preferred_element_type=jnp.float32
    )


def contract_first(left_rows, right_rows):
    return lax.dot_general(
        left_rows, right_rows, (((0,), (0,)), ((), ())), preferred_element_type=jnp.float32
    )


def segment_ids(lengths, count):
    doc_ends = jnp.cumsum(lengths)
    places = lax.broadcasted_iota(jnp.int32, (lengths.shape[0], count), 1)
    return jnp.sum((places >= doc_ends[:, None]).astype(jnp.int32), axis=0)


def head_pass(queries, keys_in, values_in, grads_in, blocks, segments):
    seq_len, head_dim = queries.shape
    block_count = seq_len // BLOCK
    select = blocks.shape[1]
    group_size = math.gcd(block_count, max(1, 512 // BLOCK))
    scale_factor = head_dim ** (-0.5)
    query_blocks = queries.reshape(block_count, BLOCK, head_dim)
    key_blocks = keys_in.reshape(block_count, BLOCK, head_dim)
    value_blocks = values_in.reshape(block_count, BLOCK, head_dim)
    grad_blocks = grads_in.reshape(block_count, BLOCK, head_dim)
    seg_blocks = segments.reshape(block_count, BLOCK)
    owner_rows = lax.broadcasted_iota(jnp.int32, (block_count, group_size * select), 0)

    def one_group(carried, group_index):
        key_acc, value_acc = carried
        first_block = group_index * group_size
        chosen = lax.dynamic_slice_in_dim(blocks, first_block, group_size, 0).reshape(-1)
        query_part = lax.dynamic_slice_in_dim(query_blocks, first_block, group_size, 0)
        grad_part = lax.dynamic_slice_in_dim(grad_blocks, first_block, group_size, 0)
        query_segs = lax.dynamic_slice_in_dim(seg_blocks, first_block, group_size, 0)
        key_part = key_blocks[chosen].reshape(group_size, select * BLOCK, head_dim)
        value_part = value_blocks[chosen].reshape(group_size, select * BLOCK, head_dim)
        key_segs = seg_blocks[chosen].reshape(group_size, select * BLOCK)
        live_mask = query_segs[:, :, None] == key_segs[:, None, :]
        scores = (
            jnp.einsum("nqd,nkd->nqk", query_part, key_part, preferred_element_type=jnp.float32)
            * scale_factor
        )
        scores = jnp.where(live_mask, scores, -1e30)
        top_score = jnp.max(scores, axis=2, keepdims=True)
        weights = jnp.where(live_mask, jnp.exp(scores - top_score), 0.0)
        soft_probs = weights / jnp.sum(weights, axis=2, keepdims=True)
        probs_bf = soft_probs.astype(jnp.bfloat16)
        attended = jnp.einsum(
            "nqk,nkd->nqd", probs_bf, value_part, preferred_element_type=jnp.float32
        ).astype(jnp.bfloat16)
        row_delta = jnp.sum(
            grad_part.astype(jnp.float32) * attended.astype(jnp.float32), axis=2, keepdims=True
        )
        d_probs = jnp.einsum(
            "nqd,nkd->nqk", grad_part, value_part, preferred_element_type=jnp.float32
        )
        d_scores = (soft_probs * (d_probs - row_delta) * scale_factor).astype(jnp.bfloat16)
        d_query = jnp.einsum(
            "nqk,nkd->nqd", d_scores, key_part, preferred_element_type=jnp.float32
        ).astype(jnp.bfloat16)
        key_terms = jnp.einsum(
            "nqk,nqd->nkd", d_scores, query_part, preferred_element_type=jnp.float32
        ).reshape(group_size * select, BLOCK * head_dim)
        value_terms = jnp.einsum(
            "nqk,nqd->nkd", probs_bf, grad_part, preferred_element_type=jnp.float32
        ).reshape(group_size * select, BLOCK * head_dim)
        owner_map = (owner_rows == chosen[None, :]).astype(jnp.float32)
        key_acc = key_acc + jnp.dot(
            owner_map,
            key_terms,
            precision=lax.Precision.HIGHEST,
            preferred_element_type=jnp.float32,
        )
        value_acc = value_acc + jnp.dot(
            owner_map,
            value_terms,
            precision=lax.Precision.HIGHEST,
            preferred_element_type=jnp.float32,
        )
        return ((key_acc, value_acc), (attended, d_query))

    blank_acc = jnp.zeros((block_count, BLOCK * head_dim), jnp.float32)
    sums, stacked = lax.scan(
        one_group, (blank_acc, blank_acc), jnp.arange(block_count // group_size, dtype=jnp.int32)
    )
    return (
        stacked[0].reshape(seq_len, head_dim),
        stacked[1].reshape(seq_len, head_dim),
        sums[0].reshape(seq_len, head_dim).astype(jnp.bfloat16),
        sums[1].reshape(seq_len, head_dim).astype(jnp.bfloat16),
    )


def per_device(tokens, w_query, w_key, w_value, w_output, grad_out, doc_lengths, block_ids):
    tok_rows = tokens[0]
    cotangent = grad_out[0]
    tok_dev, width = tok_rows.shape
    ctx_size = lax.axis_size("ctx")
    local_heads = HEADS // ctx_size
    head_band = local_heads * HEAD_DIM
    group_rows = (
        lax.all_gather(w_query, "ctx", axis=0, tiled=True),
        lax.all_gather(w_key, "ctx", axis=0, tiled=True),
        lax.all_gather(w_value, "ctx", axis=0, tiled=True),
        lax.all_gather(w_output, "ctx", axis=0, tiled=True),
    )
    pieces = (
        lax.all_gather(group_rows[0], "fsdp", axis=0, tiled=True),
        lax.all_gather(group_rows[1], "fsdp", axis=0, tiled=True),
        lax.all_gather(group_rows[2], "fsdp", axis=0, tiled=True),
        lax.all_gather(group_rows[3], "fsdp", axis=0, tiled=True),
    )
    tok_part = tok_rows
    query_acc = jnp.dot(tok_part, pieces[0], preferred_element_type=jnp.float32)
    key_acc = jnp.dot(tok_part, pieces[1], preferred_element_type=jnp.float32)
    value_acc = jnp.dot(tok_part, pieces[2], preferred_element_type=jnp.float32)
    grad_acc = contract_last(cotangent, pieces[3])
    queries = query_acc.astype(jnp.bfloat16)
    keys_all = key_acc.astype(jnp.bfloat16)
    values_all = value_acc.astype(jnp.bfloat16)
    d_attended = grad_acc.astype(jnp.bfloat16)

    def to_band(matrix):
        return matrix.reshape(tok_dev, ctx_size, head_band)

    received = (
        lax.all_to_all(to_band(queries), "ctx", split_axis=1, concat_axis=0, tiled=True),
        lax.all_to_all(to_band(keys_all), "ctx", split_axis=1, concat_axis=0, tiled=True),
        lax.all_to_all(to_band(values_all), "ctx", split_axis=1, concat_axis=0, tiled=True),
        lax.all_to_all(to_band(d_attended), "ctx", split_axis=1, concat_axis=0, tiled=True),
    )
    query_heads = received[0].reshape(-1, head_band)
    key_heads = received[1].reshape(-1, head_band)
    value_heads = received[2].reshape(-1, head_band)
    grad_heads = received[3].reshape(-1, head_band)
    seq_len = query_heads.shape[0]
    segments = segment_ids(doc_lengths[0], seq_len)
    head_base = lax.axis_index("ctx") * local_heads

    def per_head(head_index, buffers):
        column = head_index * HEAD_DIM

        def columns(matrix):
            return lax.dynamic_slice_in_dim(matrix, column, HEAD_DIM, 1)

        blocks = lax.dynamic_slice_in_dim(block_ids, head_base + head_index, 1, 0)[0]
        results = head_pass(
            columns(query_heads),
            columns(key_heads),
            columns(value_heads),
            columns(grad_heads),
            blocks,
            segments,
        )
        return (
            lax.dynamic_update_slice_in_dim(buffers[0], results[0], column, 1),
            lax.dynamic_update_slice_in_dim(buffers[1], results[1], column, 1),
            lax.dynamic_update_slice_in_dim(buffers[2], results[2], column, 1),
            lax.dynamic_update_slice_in_dim(buffers[3], results[3], column, 1),
        )

    blank_band = jnp.zeros((seq_len, head_band), jnp.bfloat16)
    buffers = lax.fori_loop(
        0, local_heads, per_head, (blank_band, blank_band, blank_band, blank_band)
    )

    def to_rows(matrix):
        return matrix.reshape(seq_len, 1, head_band)

    returned = (
        lax.all_to_all(to_rows(buffers[0]), "ctx", split_axis=0, concat_axis=1, tiled=True),
        lax.all_to_all(to_rows(buffers[1]), "ctx", split_axis=0, concat_axis=1, tiled=True),
        lax.all_to_all(to_rows(buffers[2]), "ctx", split_axis=0, concat_axis=1, tiled=True),
        lax.all_to_all(to_rows(buffers[3]), "ctx", split_axis=0, concat_axis=1, tiled=True),
    )
    attended = returned[0].reshape(tok_dev, width)
    d_query = returned[1].reshape(tok_dev, width)
    d_key = returned[2].reshape(tok_dev, width)
    d_value = returned[3].reshape(tok_dev, width)
    pieces = (
        lax.all_gather(group_rows[0], "fsdp", axis=0, tiled=True),
        lax.all_gather(group_rows[1], "fsdp", axis=0, tiled=True),
        lax.all_gather(group_rows[2], "fsdp", axis=0, tiled=True),
        lax.all_gather(group_rows[3], "fsdp", axis=0, tiled=True),
    )
    out_acc = tok_rows.astype(jnp.float32)
    att_part = attended
    out_acc = out_acc + jnp.dot(att_part, pieces[3], preferred_element_type=jnp.float32)
    update = (
        contract_last(d_query, pieces[0])
        + contract_last(d_key, pieces[1])
        + contract_last(d_value, pieces[2])
    )
    grad_acc = update
    layer_out = out_acc.astype(jnp.bfloat16)
    grad_tokens = (cotangent.astype(jnp.float32) + grad_acc).astype(jnp.bfloat16)
    total_tokens = tok_dev * lax.axis_size("dp") * lax.axis_size("fsdp") * ctx_size
    grad_scale = total_tokens ** (-0.5)
    tok_part = tok_rows
    att_part = attended
    summed = lax.psum_scatter(
        jnp.concatenate(
            [
                contract_first(tok_part, d_query),
                contract_first(tok_part, d_key),
                contract_first(tok_part, d_value),
                contract_first(att_part, cotangent),
            ],
            axis=1,
        )
        * grad_scale,
        ("fsdp", "ctx"),
        scatter_dimension=0,
        tiled=True,
    )
    summed = lax.psum(summed, "dp")
    return (
        layer_out[None],
        grad_tokens[None],
        summed[:, 0:width],
        summed[:, width : 2 * width],
        summed[:, 2 * width : 3 * width],
        summed[:, 3 * width : 4 * width],
    )


def solution(mesh):
    in_specs = (
        P(("dp", "fsdp"), "ctx", None),
        P(("fsdp", "ctx"), None),
        P(("fsdp", "ctx"), None),
        P(("fsdp", "ctx"), None),
        P(("fsdp", "ctx"), None),
        P(("dp", "fsdp"), "ctx", None),
        P(("dp", "fsdp"), None),
        P(),
    )
    out_specs = (
        P(("dp", "fsdp"), "ctx", None),
        P(("dp", "fsdp"), "ctx", None),
        P(("fsdp", "ctx"), None),
        P(("fsdp", "ctx"), None),
        P(("fsdp", "ctx"), None),
        P(("fsdp", "ctx"), None),
    )
    return jax.shard_map(
        per_device, mesh=mesh, in_specs=in_specs, out_specs=out_specs, check_vma=False
    )
```

profile of v0, /device:TPU:0, one launch (start us, length us, event | category | flops | bytes accessed | tf_op | source)
XLA Modules:
  0.0 1157.6 jit_solution(13899173250010144556)
XLA Ops:
  7.2 12.0 %all_gather.30 = bf16[256,1024]{1,0:T(8,128)(2,1)} all-gather(bf16[128,1024]{1,0:T(8,128)(2,1)} %param.16), channel_id=1, replica_groups=mesh['dp'=4,'fsdp'=4,'ctx'=2] {'ctx'}, dimensions={0}, use_global_device_ids=true | all-gather | bytes 786432 | tf_op jit(solution)/shard_map/all_gather | solution.py:121
  19.3 8.6 all_gather.34
  28.0 7.8 all_gather.28
  35.9 7.2 all_gather.32
  43.1 22.6 %all-gather.7.cloned.1.call-done = bf16[1024,1024]{1,0:T(8,128)(2,1)} async-done(((bf16[256,1024]{1,0:T(8,128)(2,1)}), bf16[1024,1024]{1,0:T(8,128)(2,1)}) %all-gather.7.cloned.1.call-update) | async-done | bytes 2097168 | tf_op jit(solution)/shard_map/all_gather | solution.py:127
  72.8 39.1 %all-gather.11.cloned.1.call-done = bf16[1024,1024]{1,0:T(8,128)(2,1)} async-done(((bf16[256,1024]{1,0:T(8,128)(2,1)}), bf16[1024,1024]{1,0:T(8,128)(2,1)}) %all-gather.11.cloned.1.call-update) | async-done | bytes 2097168 | tf_op jit(solution)/shard_map/all_gather | solution.py:126
  119.0 39.2 %all-gather.5.cloned.1.call-done = bf16[1024,1024]{1,0:T(8,128)(2,1)} async-done(((bf16[256,1024]{1,0:T(8,128)(2,1)}), bf16[1024,1024]{1,0:T(8,128)(2,1)}) %all-gather.5.cloned.1.call-update) | async-done | bytes 2097168 | tf_op jit(solution)/shard_map/all_gather | solution.py:124
  165.2 39.1 %all-gather.9.cloned.1.call-done = bf16[1024,1024]{1,0:T(8,128)(2,1)} async-done(((bf16[256,1024]{1,0:T(8,128)(2,1)}), bf16[1024,1024]{1,0:T(8,128)(2,1)}) %all-gather.9.cloned.1.call-update) | async-done | bytes 2097168 | tf_op jit(solution)/shard_map/all_gather | solution.py:125
  214.9 8.4 all-to-all-done.2
  227.1 502.9 %while.61 = (s32[]{:T(128)}, bf16[768,512]{1,0:T(8,128)(2,1)}, bf16[768,512]{1,0:T(8,128)(2,1)}, bf16[768,512]{1,0:T(8,128)(2,1)}, bf16[768,512]{1,0:T(8,128)(2,...) while((s32[]{:T(128)}, bf16[768,512]{1,0:T(8,128)(2,1)}, ...), condition=%wide.region_8.9_spmd, body=%wide.region_2.8_spmd.sunk | while | flops 295047680 | bytes 35376104 | solution.py:179
  230.6 44.1 %while.62 = (s32[]{:T(128)}, f32[6,8192]{1,0:T(8,128)S(1)}, f32[6,8192]{1,0:T(8,128)S(1)}, bf16[3,2,128,64]{2,3,1,0:T(8,128)(2,1)}, bf16[3,2,128,64]{2,3,1,0:T(8...) while((s32[]{:T(128)}, f32[6,8192]{1,0:T(8,128)S(1)}, ...), condition=%wide.region_7.7_spmd.clone, body=%wide.region_3.6_spmd.clone.sunk | while | flops 294949376 | bytes 13158382 | solution.py:99
  293.2 44.1 %while.62 = (s32[]{:T(128)}, f32[6,8192]{1,0:T(8,128)S(1)}, f32[6,8192]{1,0:T(8,128)S(1)}, bf16[3,2,128,64]{2,3,1,0:T(8,128)(2,1)}, bf16[3,2,128,64]{2,3,1,0:T(8...) while((s32[]{:T(128)}, f32[6,8192]{1,0:T(8,128)S(1)}, ...), condition=%wide.region_7.7_spmd.clone, body=%wide.region_3.6_spmd.clone.sunk | while | flops 294949376 | bytes 13158382 | solution.py:99
  357.5 44.1 %while.62 = (s32[]{:T(128)}, f32[6,8192]{1,0:T(8,128)S(1)}, f32[6,8192]{1,0:T(8,128)S(1)}, bf16[3,2,128,64]{2,3,1,0:T(8,128)(2,1)}, bf16[3,2,128,64]{2,3,1,0:T(8...) while((s32[]{:T(128)}, f32[6,8192]{1,0:T(8,128)S(1)}, ...), condition=%wide.region_7.7_spmd.clone, body=%wide.region_3.6_spmd.clone.sunk | while | flops 294949376 | bytes 13158382 | solution.py:99
  420.2 44.1 %while.62 = (s32[]{:T(128)}, f32[6,8192]{1,0:T(8,128)S(1)}, f32[6,8192]{1,0:T(8,128)S(1)}, bf16[3,2,128,64]{2,3,1,0:T(8,128)(2,1)}, bf16[3,2,128,64]{2,3,1,0:T(8...) while((s32[]{:T(128)}, f32[6,8192]{1,0:T(8,128)S(1)}, ...), condition=%wide.region_7.7_spmd.clone, body=%wide.region_3.6_spmd.clone.sunk | while | flops 294949376 | bytes 13158382 | solution.py:99
  484.5 44.1 %while.62 = (s32[]{:T(128)}, f32[6,8192]{1,0:T(8,128)S(1)}, f32[6,8192]{1,0:T(8,128)S(1)}, bf16[3,2,128,64]{2,3,1,0:T(8,128)(2,1)}, bf16[3,2,128,64]{2,3,1,0:T(8...) while((s32[]{:T(128)}, f32[6,8192]{1,0:T(8,128)S(1)}, ...), condition=%wide.region_7.7_spmd.clone, body=%wide.region_3.6_spmd.clone.sunk | while | flops 294949376 | bytes 13158382 | solution.py:99
  547.1 44.1 %while.62 = (s32[]{:T(128)}, f32[6,8192]{1,0:T(8,128)S(1)}, f32[6,8192]{1,0:T(8,128)S(1)}, bf16[3,2,128,64]{2,3,1,0:T(8,128)(2,1)}, bf16[3,2,128,64]{2,3,1,0:T(8...) while((s32[]{:T(128)}, f32[6,8192]{1,0:T(8,128)S(1)}, ...), condition=%wide.region_7.7_spmd.clone, body=%wide.region_3.6_spmd.clone.sunk | while | flops 294949376 | bytes 13158382 | solution.py:99
  611.4 44.1 %while.62 = (s32[]{:T(128)}, f32[6,8192]{1,0:T(8,128)S(1)}, f32[6,8192]{1,0:T(8,128)S(1)}, bf16[3,2,128,64]{2,3,1,0:T(8,128)(2,1)}, bf16[3,2,128,64]{2,3,1,0:T(8...) while((s32[]{:T(128)}, f32[6,8192]{1,0:T(8,128)S(1)}, ...), condition=%wide.region_7.7_spmd.clone, body=%wide.region_3.6_spmd.clone.sunk | while | flops 294949376 | bytes 13158382 | solution.py:99
  671.7 44.1 %while.62 = (s32[]{:T(128)}, f32[6,8192]{1,0:T(8,128)S(1)}, f32[6,8192]{1,0:T(8,128)S(1)}, bf16[3,2,128,64]{2,3,1,0:T(8,128)(2,1)}, bf16[3,2,128,64]{2,3,1,0:T(8...) while((s32[]{:T(128)}, f32[6,8192]{1,0:T(8,128)S(1)}, ...), condition=%wide.region_7.7_spmd.clone, body=%wide.region_3.6_spmd.clone.sunk | while | flops 294949376 | bytes 13158382 | solution.py:99
  740.6 7.5 all-to-all-done.4
  755.1 6.6 all-to-all-done.7
  768.2 5.5 all-to-all-done.6
  801.9 7.3 maximum_multiply_fusion
  813.5 278.7 %reduce-scatter.2.cloned.1.call-done = f32[128,4096]{0,1:T(8,128)} async-done(((f32[1024,4096]{0,1:T(8,128)}), f32[128,4096]{0,1:T(8,128)}) %reduce-scatter.2.cloned.1.call-update) | async-done | bytes 2097168 | tf_op jit(solution)/shard_map/reduce_scatter | solution.py:217
  1099.8 45.3 %all-reduce.2.cloned.1.call-done = f32[128,4096]{0,1:T(8,128)} async-done(((f32[128,4096]{0,1:T(8,128)}), f32[128,4096]{0,1:T(8,128)}) %all-reduce.2.cloned.1.call-update) | async-done | bytes 2097168 | tf_op jit(solution)/shard_map/psum | solution.py:232
  (1403 shorter events, 585.4 us)
Async XLA Ops:
  7.2 20.9 %copy-start.29 = (bf16[128,1024]{1,0:T(8,128)(2,1)S(1)}, bf16[128,1024]{1,0:T(8,128)(2,1)}, u32[]{:S(2)}) copy-start(bf16[128,1024]{1,0:T(8,128)(2,1)} %param.13) | copy-start | bytes 786436
  7.2 28.7 %copy-start.30 = (bf16[128,1024]{1,0:T(8,128)(2,1)S(1)}, bf16[128,1024]{1,0:T(8,128)(2,1)}, u32[]{:S(2)}) copy-start(bf16[128,1024]{1,0:T(8,128)(2,1)} %param.14) | copy-start | bytes 786436
  7.2 58.5 %all-gather.7.cloned.1.call-start = ((), (), s32[]{:S(2)}) async-start(), calls=%async_computation.10 | async-start | bytes 2621440 | tf_op jit(solution)/shard_map/all_gather | solution.py:127
  19.3 46.4 %copy-start.9 = (bf16[1,384,1024]{2,1,0:T(8,128)(2,1)S(1)}, bf16[1,384,1024]{2,1,0:T(8,128)(2,1)}, u32[]{:S(2)}) copy-start(bf16[1,384,1024]{2,1,0:T(8,128)(2,1)} %param.17) | copy-start | bytes 2359300
  19.3 92.6 %all-gather.11.cloned.1.call-start = ((), (), s32[]{:S(2)}) async-start(), calls=%async_computation.12 | async-start | bytes 2621440 | tf_op jit(solution)/shard_map/all_gather | solution.py:126
  28.0 130.2 %all-gather.5.cloned.1.call-start = ((), (), s32[]{:S(2)}) async-start(), calls=%async_computation.9 | async-start | bytes 2621440 | tf_op jit(solution)/shard_map/all_gather | solution.py:124
  35.9 168.4 %all-gather.9.cloned.1.call-start = ((), (), s32[]{:S(2)}) async-start(), calls=%async_computation.11 | async-start | bytes 2621440 | tf_op jit(solution)/shard_map/all_gather | solution.py:125
  68.3 43.6 %copy-start.2 = (bf16[1,384,1024]{2,1,0:T(8,128)(2,1)S(1)}, bf16[1,384,1024]{2,1,0:T(8,128)(2,1)}, u32[]{:S(2)}) copy-start(bf16[1,384,1024]{2,1,0:T(8,128)(2,1)} %param.12) | copy-start | bytes 2359300
  69.2 46.2 %all-to-all-start.1 = ((bf16[384,2,512]{2,0,1:T(8,128)(2,1)}), bf16[384,2,512]{2,0,1:T(8,128)(2,1)S(1)}, u32[]{:S(2)}, u32[]{:S(2)}) async-start(bf16[384,2,512]{2,0,1:T(8,128)(2,1)} %bitcast.134), calls=%async_computation.1 | async-start | bytes 1572864 | tf_op jit(solution)/shard_map/all_to_all | solution.py:146
  115.4 46.3 %all-to-all-start.3 = ((bf16[384,2,512]{2,0,1:T(8,128)(2,1)}), bf16[384,2,512]{2,0,1:T(8,128)(2,1)S(1)}, u32[]{:S(2)}, u32[]{:S(2)}) async-start(bf16[384,2,512]{2,0,1:T(8,128)(2,1)} %bitcast.132), calls=%async_computation.3 | async-start | bytes 1572864 | tf_op jit(solution)/shard_map/all_to_all | solution.py:145
  161.7 46.1 %all-to-all-start = ((bf16[384,2,512]{2,0,1:T(8,128)(2,1)}), bf16[384,2,512]{2,0,1:T(8,128)(2,1)S(1)}, u32[]{:S(2)}, u32[]{:S(2)}) async-start(bf16[384,2,512]{2,0,1:T(8,128)(2,1)} %bitcast.204), calls=%async_computation | async-start | bytes 1572864 | tf_op jit(solution)/shard_map/all_to_all | solution.py:143
  208.7 14.6 %all-to-all-start.2 = ((bf16[384,2,512]{2,0,1:T(8,128)(2,1)}), bf16[384,2,512]{2,0,1:T(8,128)(2,1)S(1)}, u32[]{:S(2)}, u32[]{:S(2)}) async-start(bf16[384,2,512]{2,0,1:T(8,128)(2,1)} %bitcast.133), calls=%async_computation.2 | async-start | bytes 1572864 | tf_op jit(solution)/shard_map/all_to_all | solution.py:144
  337.3 16.7 %copy-start.6 = (bf16[768,512]{1,0:T(8,128)(2,1)S(1)}, bf16[768,512]{1,0:T(8,128)(2,1)}, u32[]{:S(2)}) copy-start(bf16[768,512]{1,0:T(8,128)(2,1)} %copy-done.5) | copy-start | bytes 2359300 | tf_op jit(solution)/shard_map/while
  337.4 16.7 %copy-start.8 = (bf16[768,512]{1,0:T(8,128)(2,1)S(1)}, bf16[768,512]{1,0:T(8,128)(2,1)}, u32[]{:S(2)}) copy-start(bf16[768,512]{1,0:T(8,128)(2,1)} %copy-done.7) | copy-start | bytes 2359300 | tf_op jit(solution)/shard_map/while
  464.3 16.7 %copy-start.6 = (bf16[768,512]{1,0:T(8,128)(2,1)S(1)}, bf16[768,512]{1,0:T(8,128)(2,1)}, u32[]{:S(2)}) copy-start(bf16[768,512]{1,0:T(8,128)(2,1)} %copy-done.5) | copy-start | bytes 2359300 | tf_op jit(solution)/shard_map/while
  464.3 16.7 %copy-start.8 = (bf16[768,512]{1,0:T(8,128)(2,1)S(1)}, bf16[768,512]{1,0:T(8,128)(2,1)}, u32[]{:S(2)}) copy-start(bf16[768,512]{1,0:T(8,128)(2,1)} %copy-done.7) | copy-start | bytes 2359300 | tf_op jit(solution)/shard_map/while
  464.3 16.7 %copy-start.24 = (bf16[768,512]{0,1:T(8,128)(2,1)S(1)}, bf16[768,512]{0,1:T(8,128)(2,1)}, u32[]{:S(2)}) copy-start(bf16[768,512]{0,1:T(8,128)(2,1)} %copy-done.23) | copy-start | bytes 2359300 | tf_op jit(solution)/shard_map/while
  591.3 16.7 %copy-start.6 = (bf16[768,512]{1,0:T(8,128)(2,1)S(1)}, bf16[768,512]{1,0:T(8,128)(2,1)}, u32[]{:S(2)}) copy-start(bf16[768,512]{1,0:T(8,128)(2,1)} %copy-done.5) | copy-start | bytes 2359300 | tf_op jit(solution)/shard_map/while
  734.4 13.7 %all-to-all-start.4 = ((bf16[2,2,98304]{2,1,0:T(2,128)(2,1)}), bf16[2,2,98304]{2,1,0:T(2,128)(2,1)S(1)}, u32[]{:S(2)}, u32[]{:S(2)}) async-start(bf16[2,2,98304]{2,1,0:T(2,128)(2,1)} %reshape.260), calls=%async_computation.4 | async-start | bytes 1572864 | tf_op jit(solution)/shard_map/all_to_all | solution.py:187
  748.1 13.7 %all-to-all-start.7 = ((bf16[2,2,98304]{2,1,0:T(2,128)(2,1)}), bf16[2,2,98304]{2,1,0:T(2,128)(2,1)}, u32[]{:S(2)}, u32[]{:S(2)}) async-start(bf16[2,2,98304]{2,1,0:T(2,128)(2,1)} %reshape.262), calls=%async_computation.7 | async-start | bytes 1572864 | tf_op jit(solution)/shard_map/all_to_all | solution.py:190
  761.8 11.9 %all-to-all-start.6 = ((bf16[2,2,98304]{2,1,0:T(2,128)(2,1)}), bf16[2,2,98304]{2,1,0:T(2,128)(2,1)S(1)}, u32[]{:S(2)}, u32[]{:S(2)}) async-start(bf16[2,2,98304]{2,1,0:T(2,128)(2,1)} %reshape.266), calls=%async_computation.6 | async-start | bytes 1572864 | tf_op jit(solution)/shard_map/all_to_all | solution.py:189
  773.6 16.5 %all-to-all-start.5 = ((bf16[2,2,98304]{2,1,0:T(2,128)(2,1)}), bf16[2,2,98304]{2,1,0:T(2,128)(2,1)}, u32[]{:S(2)}, u32[]{:S(2)}) async-start(bf16[2,2,98304]{2,1,0:T(2,128)(2,1)} %reshape.264), calls=%async_computation.5 | async-start | bytes 1572864 | tf_op jit(solution)/shard_map/all_to_all | solution.py:188
  778.0 314.3 %reduce-scatter.2.cloned.1.call-start = ((), (), s32[]{:S(2)}) async-start(), calls=%async_computation.13 | async-start | bytes 18874368 | tf_op jit(solution)/shard_map/reduce_scatter | solution.py:217
  809.2 335.9 %all-reduce.2.cloned.1.call-start = ((), (), s32[]{:S(2)}) async-start(), calls=%async_computation.14 | async-start | bytes 4194304 | tf_op jit(solution)/shard_map/psum | solution.py:232
  (298 other events, 1089.1 us)
Sparse Core Ops, SparseCore 0:
  19.4 46.2 all-gather.6
  67.2 44.6 all-gather.10
  113.5 44.6 all-gather.4
  159.6 44.6 all-gather.8
  809.3 282.9 reduce-scatter.1
  1094.6 50.4 all-reduce.1
where the time goes:
time: 1170 us; the launch traced here: 1160 us
  waiting for transfers between devices  492 us (42%)
  local copies, waits for them, and re-layouts  327 us (28%)
  matrix products  221 us (19%)
  blocking collectives  35.6 us (3%)
  starting transfers between devices  30.8 us (3%)
  loops' own time  22.7 us (2%)
  other arithmetic  14.6 us (1%)
  between operations  14.6 us (1%)
    reduce_scatter x1, waiting for transfers between devices, per_device(): lax.psum_scatter(jnp.concatenate([contract_first(tok_part, d_query), cont...  279 us
    psum x1, waiting for transfers between devices, per_device(): summed = lax.psum(summed, 'dp')  45.3 us
    dot_general x24, matrix products, one_group(): jnp.einsum('nqk,nqd->nkd', probs_bf, grad_part, preferred_element_type=jn...  43.8 us
    all_gather x1, waiting for transfers between devices, per_device(): lax.all_gather(group_rows[0], 'fsdp', axis=0, tiled=True)  39.2 us
    all_gather x1, waiting for transfers between devices, per_device(): lax.all_gather(group_rows[2], 'fsdp', axis=0, tiled=True)  39.1 us
    all_gather x1, waiting for transfers between devices, per_device(): lax.all_gather(group_rows[1], 'fsdp', axis=0, tiled=True)  39.1 us
    dot_general x24, matrix products, one_group(): jnp.einsum('nqd,nkd->nqk', grad_part, value_part, preferred_element_type=...  38.3 us
    sub x24, matrix products, one_group(): weights = jnp.where(live_mask, jnp.exp(scores - top_score), 0.0)  37.5 us
  transfers between devices with their start and end apart: 14, of which 10 were waited for; matrix products, arithmetic and copies ran while one was open for 4% of the time, Pallas kernels for 0%

commit v1 on v0

--- a/solution.py
+++ b/solution.py
@@ -3,6 +3,8 @@
 import jax
 import jax.numpy as jnp
 from jax import lax
+from jax.experimental import pallas as pl
+from jax.experimental.pallas import tpu as pltpu
 from jax.sharding import PartitionSpec as P
 
 HEADS = 16
@@ -107,7 +109,7 @@
     )
 
 
-def per_device(tokens, w_query, w_key, w_value, w_output, grad_out, doc_lengths, block_ids):
+def general_device(tokens, w_query, w_key, w_value, w_output, grad_out, doc_lengths, block_ids):
     tok_rows = tokens[0]
     cotangent = grad_out[0]
     tok_dev, width = tok_rows.shape
@@ -240,6 +242,204 @@
     )
 
 
+def attention_kernel(
+    logs_ref, seg_row_ref, seg_col_ref, q_ref, k_ref, v_ref, g_ref,
+    att_ref, dq_ref, dk_ref, dv_ref, dk_acc, dv_acc,
+):
+    seq_len, lanes = q_ref.shape
+    heads_here = lanes // HEAD_DIM
+    block_count = seq_len // BLOCK
+    tile = BLOCK * (2 if block_count % 2 == 0 else 1)
+    scale_factor = HEAD_DIM ** (-0.5)
+    lane_ids = lax.broadcasted_iota(jnp.int32, (1, lanes), 1) // HEAD_DIM
+    keys = k_ref[...]
+    values = v_ref[...]
+    dk_acc[...] = jnp.zeros_like(dk_acc)
+    dv_acc[...] = jnp.zeros_like(dv_acc)
+    seg_keys = seg_col_ref[...]
+    zero = jnp.zeros((), jnp.bfloat16)
+
+    for part in range(seq_len // tile):
+        rows = pl.ds(part * tile, tile)
+        query_part = q_ref[rows, :] * jnp.asarray(scale_factor, jnp.bfloat16)
+        grad_part = g_ref[rows, :]
+        live = seg_keys == seg_row_ref[:, rows]
+        att_sum = jnp.zeros((tile, lanes), jnp.float32)
+        dq_sum = jnp.zeros((tile, lanes), jnp.float32)
+        for head in range(heads_here):
+            mine = lane_ids == head
+            q_head = jnp.where(mine, query_part, zero)
+            g_head = jnp.where(mine, grad_part, zero)
+            scores = contract_last(keys, q_head)
+            bias = jnp.broadcast_to(
+                logs_ref[head, :, rows][:, None, :], (block_count, BLOCK, tile)
+            ).reshape(seq_len, tile)
+            scores = jnp.where(live, scores + bias, -1e30)
+            top_score = jnp.max(scores, axis=0, keepdims=True)
+            weights = jnp.exp(scores - top_score)
+            inverse = 1.0 / jnp.sum(weights, axis=0, keepdims=True)
+            probs = weights * inverse
+            d_probs = contract_last(values, g_head)
+            row_delta = jnp.sum(probs * d_probs, axis=0, keepdims=True)
+            probs_bf = probs.astype(jnp.bfloat16)
+            d_scores = (probs * (d_probs - row_delta)).astype(jnp.bfloat16)
+            att_sum = jnp.where(mine, contract_first(probs_bf, values), att_sum)
+            dq_sum = jnp.where(mine, contract_first(d_scores, keys), dq_sum)
+            dv_acc[...] += jnp.dot(probs_bf, g_head, preferred_element_type=jnp.float32)
+            dk_acc[...] += jnp.dot(d_scores, q_head, preferred_element_type=jnp.float32)
+        att_ref[rows, :] = att_sum.astype(jnp.bfloat16)
+        dq_ref[rows, :] = (dq_sum * scale_factor).astype(jnp.bfloat16)
+    dk_ref[...] = dk_acc[...].astype(jnp.bfloat16)
+    dv_ref[...] = dv_acc[...].astype(jnp.bfloat16)
+
+
+def attention(queries, keys, values, grads, logs, segments, stripe):
+    seq_len, band = queries.shape
+    heads_here = stripe // HEAD_DIM
+    block_count = logs.shape[1]
+    whole = pl.BlockSpec((seq_len, stripe), lambda i: (0, i))
+    return pl.pallas_call(
+        attention_kernel,
+        grid=(band // stripe,),
+        out_shape=[jax.ShapeDtypeStruct((seq_len, band), jnp.bfloat16)] * 4,
+        in_specs=[
+            pl.BlockSpec((heads_here, block_count, seq_len), lambda i: (i, 0, 0)),
+            pl.BlockSpec((1, seq_len), lambda i: (0, 0)),
+            pl.BlockSpec((seq_len, 1), lambda i: (0, 0)),
+            whole, whole, whole, whole,
+        ],
+        out_specs=[whole] * 4,
+        scratch_shapes=[pltpu.VMEM((seq_len, stripe), jnp.float32)] * 2,
+        compiler_params=pltpu.CompilerParams(vmem_limit_bytes=48 * 1024 * 1024),
+        name="attention",
+    )(logs, segments[None, :], segments[:, None], queries, keys, values, grads)
+
+
+def block_logs(blocks, seq_len):
+    block_count = blocks.shape[1]
+    ids = jnp.arange(block_count, dtype=jnp.int32)
+    counts = jnp.sum((blocks[:, None, :, :] == ids[None, :, None, None]).astype(jnp.float32), 3)
+    logs = jnp.where(counts > 0, jnp.log(jnp.maximum(counts, 1.0)), -1e30)
+    return jnp.repeat(logs, seq_len // block_count, axis=2)
+
+
+def striped_device(tokens, w_query, w_key, w_value, w_output, grad_out, doc_lengths, block_ids):
+    tok_rows = tokens[0]
+    cotangent = grad_out[0]
+    tok_dev, width = tok_rows.shape
+    rows = w_query.shape[0]
+    dp_size, fsdp_size = lax.axis_size("dp"), lax.axis_size("fsdp")
+    ctx_size = 2
+    me = lax.axis_index("ctx")
+    swap = [(0, 1), (1, 0)]
+    band = fsdp_size * rows
+    seq_len = tok_dev * ctx_size
+    share = rows // dp_size
+
+    def other(matrix):
+        return lax.ppermute(matrix, "ctx", swap)
+
+    def ordered(own, peer):
+        first = me == 0
+        return jnp.stack([jnp.where(first, own, peer), jnp.where(first, peer, own)])
+
+    tok_peer = other(tok_rows)
+    cot_peer = other(cotangent)
+
+    start = lax.axis_index("dp") * share
+
+    def my_share(matrix):
+        return lax.dynamic_slice_in_dim(matrix, start, share, 0)
+
+    qkv = jnp.stack([my_share(w_query), my_share(w_key), my_share(w_value)], axis=1)
+    qkv = qkv.reshape(share, 3, fsdp_size, ctx_size, rows)
+    kept = lax.dynamic_index_in_dim(qkv, me, 3, False).reshape(share, 3 * band)
+    sent = lax.dynamic_index_in_dim(qkv, 1 - me, 3, False).reshape(share, 3 * band)
+    qkv = ordered(kept, other(sent))
+    out_share = my_share(w_output).reshape(share, ctx_size, width // 2).transpose(1, 0, 2)
+    packed = jnp.concatenate([qkv, out_share], axis=2)
+    gathered = lax.all_gather(packed, ("fsdp", "dp"), axis=0, tiled=False)
+    gathered = gathered.reshape(fsdp_size, dp_size, ctx_size, share, 3 * band + width // 2)
+    w_qkv = gathered[..., : 3 * band].transpose(0, 2, 1, 3, 4).reshape(width, 3 * band)
+    w_out = gathered[..., 3 * band :].transpose(0, 1, 3, 2, 4).reshape(band, width)
+
+    tok_all = ordered(tok_rows, tok_peer).reshape(seq_len, width)
+    cot_all = ordered(cotangent, cot_peer).reshape(seq_len, width)
+    queries = jnp.dot(
+        tok_all, w_qkv[:, :band], preferred_element_type=jnp.float32
+    ).astype(jnp.bfloat16)
+    keys = jnp.dot(
+        tok_all, w_qkv[:, band : 2 * band], preferred_element_type=jnp.float32
+    ).astype(jnp.bfloat16)
+    values = jnp.dot(
+        tok_all, w_qkv[:, 2 * band :], preferred_element_type=jnp.float32
+    ).astype(jnp.bfloat16)
+    d_attended = contract_last(cot_all, w_out).astype(jnp.bfloat16)
+
+    segments = segment_ids(doc_lengths[0], seq_len)
+    stripe_heads = rows // HEAD_DIM
+    my_blocks = lax.dynamic_index_in_dim(
+        block_ids.reshape((fsdp_size, ctx_size, stripe_heads) + block_ids.shape[1:]), me, 1, False
+    ).reshape((fsdp_size * stripe_heads,) + block_ids.shape[1:])
+    logs = block_logs(my_blocks, seq_len)
+    attended, d_query, d_key, d_value = attention(
+        queries, keys, values, d_attended, logs, segments, rows
+    )
+    d_qkv = jnp.concatenate([d_query, d_key, d_value], axis=1)
+
+    total_tokens = tok_dev * dp_size * fsdp_size * ctx_size
+    grad_scale = total_tokens ** (-0.5)
+    g_qkv = (contract_first(tok_all, d_qkv) * grad_scale).astype(jnp.bfloat16)
+    g_out = (contract_first(attended, cot_all) * grad_scale).astype(jnp.bfloat16)
+    g_qkv = g_qkv.reshape(fsdp_size, ctx_size, dp_size, share, 3 * band).transpose(2, 0, 1, 3, 4)
+    g_out = g_out.reshape(fsdp_size, dp_size, share, ctx_size, width // 2).transpose(1, 0, 3, 2, 4)
+    partial = jnp.concatenate([g_qkv, g_out], axis=4)
+    summed = lax.psum_scatter(partial, "dp", scatter_dimension=0, tiled=False)
+    summed = lax.psum_scatter(summed, "fsdp", scatter_dimension=0, tiled=False)
+    s_qkv = summed[..., : 3 * band]
+    kept = lax.dynamic_index_in_dim(s_qkv, me, 0, False)
+    sent = lax.dynamic_index_in_dim(s_qkv, 1 - me, 0, False)
+    final = jnp.concatenate([ordered(kept, other(sent)), summed[..., 3 * band :]], axis=2)
+    final = lax.all_gather(final, "dp", axis=0, tiled=False)
+    f_qkv = final[..., : 3 * band].reshape(dp_size, ctx_size, share, 3, fsdp_size, rows)
+    f_qkv = f_qkv.transpose(3, 0, 2, 4, 1, 5).reshape(3, rows, width).astype(jnp.float32)
+    f_out = final[..., 3 * band :].transpose(0, 2, 1, 3).reshape(rows, width).astype(jnp.float32)
+
+    out_part = jnp.dot(attended, w_out, preferred_element_type=jnp.float32)
+    tok_part = contract_last(d_qkv, w_qkv)
+    out_part = out_part.reshape(ctx_size, tok_dev, width)
+    tok_part = tok_part.reshape(ctx_size, tok_dev, width)
+
+    def pick(matrix, index):
+        return lax.dynamic_index_in_dim(matrix, index, 0, False)
+
+    out_sent = other(pick(out_part, 1 - me).astype(jnp.bfloat16))
+    tok_sent = other(pick(tok_part, 1 - me).astype(jnp.bfloat16))
+    layer_out = tok_rows.astype(jnp.float32) + pick(out_part, me) + out_sent.astype(jnp.float32)
+    grad_tokens = cotangent.astype(jnp.float32) + pick(tok_part, me) + tok_sent.astype(jnp.float32)
+    return (
+        layer_out.astype(jnp.bfloat16)[None],
+        grad_tokens.astype(jnp.bfloat16)[None],
+        f_qkv[0],
+        f_qkv[1],
+        f_qkv[2],
+        f_out,
+    )
+
+
+def per_device(tokens, w_query, w_key, w_value, w_output, grad_out, doc_lengths, block_ids):
+    rows = w_query.shape[0]
+    dp_size = lax.axis_size("dp")
+    striped = (
+        lax.axis_size("ctx") == 2
+        and rows % 128 == 0
+        and rows % HEAD_DIM == 0
+        and rows % (dp_size * 16) == 0
+    )
+    body = striped_device if striped else general_device
+    return body(tokens, w_query, w_key, w_value, w_output, grad_out, doc_lengths, block_ids)
+
+
 def solution(mesh):
     in_specs = (
         P(("dp", "fsdp"), "ctx", None),

time: 1170 us -> 261 us (0.22)
  waiting for transfers between devices: 492 us -> 153 us
  local copies, waits for them, and re-layouts: 327 us -> 29.8 us
  matrix products: 221 us -> 16.9 us
  blocking collectives: 35.6 us -> 0 us
  Pallas kernels: 0 us -> 27.6 us
  loops' own time: 22.7 us -> 0 us
  starting transfers between devices: 30.8 us -> 8.95 us
    reduce_scatter x1 -> x2, waiting for transfers between devices: 279 us -> 72.7 us  [the longest x1 43.1 us: striped_device(): summed = lax.psum_scatter(partial, 'dp', scatter_dimension=0, tiled=False)]
    dot_general x172 -> x4, matrix products: 167 us -> 3.9 us  [the longest x1 0.98 us: striped_device(): out_part = jnp.dot(attended, w_out, preferred_element_type=jnp.float32)]
    all_gather x4 -> x2, waiting for transfers between devices: 140 us -> 15.9 us  [the longest x1 15.9 us: striped_device(): gathered = lax.all_gather(packed, ('fsdp', 'dp'), axis=0, tiled=False)]
    dynamic_update_slice x56 -> x0, local copies, waits for them, and re-layouts: 122 us -> none  [the longest x8 26.9 us: per_head(): lax.dynamic_update_slice_in_dim(buffers[3], results[3], column, 1)]
    ppermute x0 -> x6, waiting for transfers between devices: none -> 64.1 us  [other(): return lax.ppermute(matrix, 'ctx', swap)]
    dynamic_slice x112 -> x6, local copies, waits for them, and re-layouts: 48.9 us -> 3.1 us  [the longest x2 1.88 us: my_share(): return lax.dynamic_slice_in_dim(matrix, start, share, 0)]
    psum x1 -> x0, waiting for transfers between devices: 45.3 us -> none  [per_device(): summed = lax.psum(summed, 'dp')]
    gather x72 -> x0, local copies, waits for them, and re-layouts: 44.6 us -> none  [the longest x24 15.5 us: one_group(): key_part = key_blocks[chosen].reshape(group_size, select * BLOCK, head_dim)]
  transfers between devices with their start and end apart: 14 -> 10, of which waited for: 10 -> 8; matrix products, arithmetic and copies ran while one was open for 4% -> 7% of each run, Pallas kernels for 0% -> 0%
where the time goes in v1:
time: 261 us; the launch traced here: 260 us
  waiting for transfers between devices  153 us (59%)
  local copies, waits for them, and re-layouts  29.8 us (11%)
  Pallas kernels  27.6 us (11%)
  matrix products  16.9 us (6%)
  between operations  14.2 us (5%)
  other arithmetic  9.96 us (4%)
  starting transfers between devices  8.95 us (3%)
    ppermute x6, waiting for transfers between devices, other(): return lax.ppermute(matrix, 'ctx', swap)  64.1 us
    reduce_scatter x1, waiting for transfers between devices, striped_device(): summed = lax.psum_scatter(partial, 'dp', scatter_dimension=0, tiled=False)  43.1 us
    reduce_scatter x1, waiting for transfers between devices, striped_device(): summed = lax.psum_scatter(summed, 'fsdp', scatter_dimension=0, tiled=False)  29.5 us
    pallas_call x1, Pallas kernels, attention(): pl.pallas_call(attention_kernel, grid=(band // stripe,), out_shape=[jax.S...  27.6 us
    all_gather x1, waiting for transfers between devices, striped_device(): gathered = lax.all_gather(packed, ('fsdp', 'dp'), axis=0, tiled=False)  15.9 us
    ppermute x6, starting transfers between devices, other(): return lax.ppermute(matrix, 'ctx', swap)  8.79 us
    dot_general x2, matrix products, contract_last(): lax.dot_general(left_rows, right_rows, (((1,), (1,)), ((), ())), preferre...  8.07 us
  transfers between devices with their start and end apart: 10, of which 8 were waited for; matrix products, arithmetic and copies ran while one was open for 7% of the time, Pallas kernels for 0%

profile of v1, /device:TPU:0, one launch (start us, length us, event | category | flops | bytes accessed | tf_op | source)
XLA Modules:
  0.0 260.1 jit_solution(872767963367515497)
XLA Ops:
  10.0 3.0 %collective-permute-start.1 = (bf16[32,1536]{1,0:T(8,128)(2,1)S(1)}, bf16[32,1536]{1,0:T(8,128)(2,1)S(1)}, u32[]{:S(2)}, u32[]{:S(2)}) collective-permute-start(bf16[32,1536]{1,0:T(8,128)(2,1)S(1)} %reshape.109), channel_id=1, source_target_pairs={{0,1},{1,0},{2,3},{3,2},{4,5},{5,4},{6,7},{7,6},{8,9},{9,8},{10,11... | collective-permute-start | bytes 294920 | tf_op jit(solution)/shard_map/ppermute | solution.py:340
  13.1 2.7 %collective-permute-done.1 = bf16[32,1536]{1,0:T(8,128)(2,1)S(1)} collective-permute-done((bf16[32,1536]{1,0:T(8,128)(2,1)S(1)}, bf16[32,1536]{1,0:T(8,128)(2,1)S(1)}, u32[]{:S(2)}, u32[]{:S(2)}) %collective-permute-start.1) | collective-permute-done | bytes 98336 | tf_op jit(solution)/shard_map/ppermute | solution.py:340
  16.6 1.9 collective-permute-start.2
  19.2 1.4 copy.74
  22.3 14.9 %collective-permute-done.2 = bf16[384,1024]{1,0:T(8,128)(2,1)S(1)} collective-permute-done((bf16[384,1024]{1,0:T(8,128)(2,1)S(1)}, bf16[384,1024]{1,0:T(8,128)(2,1)S(1)}, u32[]{:S(2)}, u32[]{:S(2)}) %collective-permute-start.2) | collective-permute-done | bytes 786464 | tf_op jit(solution)/shard_map/ppermute | solution.py:340
  37.2 15.1 %collective-permute-done = bf16[384,1024]{1,0:T(8,128)(2,1)S(1)} collective-permute-done((bf16[384,1024]{1,0:T(8,128)(2,1)S(1)}, bf16[384,1024]{1,0:T(8,128)(2,1)S(1)}, u32[]{:S(2)}, u32[]{:S(2)}) %collective-permute-start) | collective-permute-done | bytes 786464 | tf_op jit(solution)/shard_map/ppermute | solution.py:340
  52.9 15.9 %all-gather.5.cloned.1.call-done = bf16[32,32,2048]{2,1,0:T(8,128)(2,1)} async-done(((bf16[2,32,2048]{2,1,0:T(8,128)(2,1)}), bf16[32,32,2048]{2,1,0:T(8,128)(2,1)}) %all-gather.5.cloned.1.call-update) | async-done | bytes 4194320 | tf_op jit(solution)/shard_map/all_gather | solution.py:361
  68.8 1.3 slice_bitcast_fusion.1
  70.1 2.2 slice_bitcast_fusion
  77.7 1.9 convolution_convert_fusion.g_ref
  79.7 27.6 %attention.1 = (bf16[768,512]{1,0:T(8,128)(2,1)S(1)}, bf16[768,512]{1,0:T(8,128)(2,1)S(1)}, bf16[768,512]{1,0:T(8,128)(2,1)S(1)}, bf16[768,512]{1,0:T(8,128)(2,1)S(1)}) custom-call(f32[8,6,768]{2,1,0:T(8,128)S(1)} %copy-done, s32[1,768]{1,0:T(1,128)S(1)} %broadcast_in_dim.23.seg_row_ref, s32[768,1]{1,0:T(8,128)S(1)} %broadcast_in_dim.27.seg_col_ref, ...), custom_call_target="tpu_custom_call" | custom-call | tf_op jit(solution)/shard_map/attention/pallas_call | solution.py:301
  107.3 2.0 multiply_convert_fusion.1
  109.2 2.6 %reshape.116 = bf16[4,4,32,2,512]{4,3,2,1,0:T(2,128)(2,1)} reshape(bf16[512,1024]{1,0:T(8,128)(2,1)} %multiply_convert_fusion.1) | data formatting | bytes 2097152 | tf_op jit(solution)/shard_map/reshape | solution.py:395
  111.9 1.4 copy.95
  114.7 2.9 %multiply_convert_fusion = bf16[1024,1536]{1,0:T(8,128)(2,1)S(1)} fusion(bf16[768,1024]{1,0:T(8,128)(2,1)S(1)} %bitcast.138, bf16[768,1536]{1,0:T(8,128)(2,1)S(1)} %constant_dynamic-update-slice_fusion.3), kind=kOutput, calls=%fused_computation | convolution fusion | flops 2419064832 | bytes 7077888 | tf_op jit(solution)/shard_map/dot_general | solution.py:22
  117.9 2.6 %pad_maximum_fusion = bf16[4,4,2,32,2048]{4,3,2,1,0:T(8,128)(2,1)} fusion(bf16[4,4,2,32,512]{4,3,2,1,0:T(8,128)(2,1)S(1)} %bitcast.126, bf16[4,4,2,32,1536]{4,3,2,1,0:T(8,128)(2,1)S(1)} %bitcast.121), kind=kLoop, calls=%fused_computation.1 | loop fusion | flops 8388608 | bytes 8388608 | tf_op jit(solution)/shard_map/concatenate | solution.py:396
  120.6 43.1 %reduce-scatter.3.cloned.1.call-done = bf16[1,4,2,32,2048]{4,3,2,1,0:T(8,128)(2,1)} async-done(((bf16[4,4,2,32,2048]{4,3,2,1,0:T(8,128)(2,1)}), bf16[1,4,2,32,2048]{4,3,2,1,0:T(8,128)(2,1)}) %reduce-scatter.3.cloned.1.call-update) | async-done | bytes 1048592 | tf_op jit(solution)/shard_map/reduce_scatter | solution.py:397
  163.8 29.5 %reduce-scatter.5.cloned.1.call-done = bf16[1,2,32,2048]{3,2,1,0:T(8,128)(2,1)} async-done(((bf16[4,2,32,2048]{3,2,1,0:T(8,128)(2,1)}), bf16[1,2,32,2048]{3,2,1,0:T(8,128)(2,1)}) %reduce-scatter.5.cloned.1.call-update) | async-done | bytes 262160 | tf_op jit(solution)/shard_map/reduce_scatter | solution.py:398
  194.3 1.5 collective-permute-start.5
  195.8 6.1 %fusion.15 = f32[2,384,1024]{2,1,0:T(8,128)} fusion(bf16[2,384,1536]{2,1,0:T(8,128)(2,1)S(1)} %bitcast.146, bf16[1024,1536,1]{1,0,2:T(8,128)(2,1)} %bitcast.130), kind=kOutput, calls=%fused_computation.65 | convolution fusion | flops 2415919104 | bytes 8650752 | tf_op jit(solution)/shard_map/dot_general | solution.py:16
  203.6 2.4 fusion.8
  208.6 1.5 collective-permute-start.3
  210.1 17.5 %collective-permute-done.4 = bf16[384,1024]{1,0:T(8,128)(2,1)S(1)} collective-permute-done((bf16[384,1024]{1,0:T(8,128)(2,1)}, bf16[384,1024]{1,0:T(8,128)(2,1)S(1)}, u32[]{:S(2)}, u32[]{:S(2)}) %collective-permute-start.4) | collective-permute-done | bytes 786464 | tf_op jit(solution)/shard_map/ppermute | solution.py:340
  228.9 13.9 %collective-permute-done.3 = bf16[384,1024]{1,0:T(8,128)(2,1)S(1)} collective-permute-done((bf16[384,1024]{1,0:T(8,128)(2,1)S(1)}, bf16[384,1024]{1,0:T(8,128)(2,1)S(1)}, u32[]{:S(2)}, u32[]{:S(2)}) %collective-permute-start.3) | collective-permute-done | bytes 786464 | tf_op jit(solution)/shard_map/ppermute | solution.py:340
  (104 shorter events, 30.7 us)
Async XLA Ops:
  7.2 9.4 %copy-start.4 = (bf16[1,384,1024]{2,1,0:T(8,128)(2,1)S(1)}, bf16[1,384,1024]{2,1,0:T(8,128)(2,1)}, u32[]{:S(2)}) copy-start(bf16[1,384,1024]{2,1,0:T(8,128)(2,1)} %param.13) | copy-start | bytes 2359300
  7.2 11.3 %copy-start.6 = (bf16[1,384,1024]{2,1,0:T(8,128)(2,1)S(1)}, bf16[1,384,1024]{2,1,0:T(8,128)(2,1)}, u32[]{:S(2)}) copy-start(bf16[1,384,1024]{2,1,0:T(8,128)(2,1)} %param.8) | copy-start | bytes 2359300
  7.2 11.5 %copy-start.15 = (s32[1,8]{1,0:T(1,128)S(1)}, s32[1,8]{1,0:T(1,128)}, u32[]{:S(2)}) copy-start(s32[1,8]{1,0:T(1,128)} %param.14) | copy-start | bytes 100
  7.2 61.6 %all-gather.5.cloned.1.call-start = ((), (), s32[]{:S(2)}) async-start(), calls=%async_computation.4 | async-start | bytes 4456448 | tf_op jit(solution)/shard_map/all_gather | solution.py:361
  10.0 5.8 %collective-permute-start.1 = (bf16[32,1536]{1,0:T(8,128)(2,1)S(1)}, bf16[32,1536]{1,0:T(8,128)(2,1)S(1)}, u32[]{:S(2)}, u32[]{:S(2)}) collective-permute-start(bf16[32,1536]{1,0:T(8,128)(2,1)S(1)} %reshape.109), channel_id=1, source_target_pairs={{0,1},{1,0},{2,3},{3,2},{4,5},{5,4},{6,7},{7,6},{8,9},{9,8},{10,11... | collective-permute-start | bytes 294920 | tf_op jit(solution)/shard_map/ppermute | solution.py:340
  16.6 147.2 %reduce-scatter.3.cloned.1.call-start = ((), (), s32[]{:S(2)}) async-start(), calls=%async_computation.2 | async-start | bytes 5242880 | tf_op jit(solution)/shard_map/reduce_scatter | solution.py:397
  16.6 20.5 %collective-permute-start.2 = (bf16[384,1024]{1,0:T(8,128)(2,1)S(1)}, bf16[384,1024]{1,0:T(8,128)(2,1)S(1)}, u32[]{:S(2)}, u32[]{:S(2)}) collective-permute-start(bf16[384,1024]{1,0:T(8,128)(2,1)S(1)} %bitcast.132), channel_id=1, source_target_pairs={{0,1},{1,0},{2,3},{3,2},{4,5},{5,4},{6,7},{7,6},{8,9},{9,8},{10,11... | collective-permute-start | bytes 2359304 | tf_op jit(solution)/shard_map/ppermute | solution.py:340
  18.5 33.8 %collective-permute-start = (bf16[384,1024]{1,0:T(8,128)(2,1)S(1)}, bf16[384,1024]{1,0:T(8,128)(2,1)S(1)}, u32[]{:S(2)}, u32[]{:S(2)}) collective-permute-start(bf16[384,1024]{1,0:T(8,128)(2,1)S(1)} %bitcast.133), channel_id=1, source_target_pairs={{0,1},{1,0},{2,3},{3,2},{4,5},{5,4},{6,7},{7,6},{8,9},{9,8},{10,11... | collective-permute-start | bytes 2359304 | tf_op jit(solution)/shard_map/ppermute | solution.py:340
  52.8 24.2 %copy-start.11 = (bf16[2,384,1024]{2,1,0:T(8,128)(2,1)}, bf16[2,384,1024]{2,1,0:T(8,128)(2,1)S(1)}, u32[]{:S(2)}) copy-start(bf16[2,384,1024]{2,1,0:T(8,128)(2,1)S(1)} %pad_maximum_fusion.2) | copy-start | bytes 4718596
  52.9 21.7 %copy-start.9 = (bf16[2,384,1024]{2,1,0:T(8,128)(2,1)}, bf16[2,384,1024]{2,1,0:T(8,128)(2,1)S(1)}, u32[]{:S(2)}) copy-start(bf16[2,384,1024]{2,1,0:T(8,128)(2,1)S(1)} %pad_maximum_fusion.1) | copy-start | bytes 4718596
  72.7 2.0 copy-start.3
  77.7 1.9 copy-start
  79.7 27.6 %copy-start.12 = (bf16[2,384,1024]{2,1,0:T(8,128)(2,1)S(1)}, bf16[2,384,1024]{2,1,0:T(8,128)(2,1)}, u32[]{:S(2)}) copy-start(bf16[2,384,1024]{2,1,0:T(8,128)(2,1)} %copy-done.11) | copy-start | bytes 4718596
  114.7 2.9 %copy-start.13 = (bf16[768,1536]{1,0:T(8,128)(2,1)}, bf16[768,1536]{1,0:T(8,128)(2,1)S(1)}, u32[]{:S(2)}) copy-start(bf16[768,1536]{1,0:T(8,128)(2,1)S(1)} %constant_dynamic-update-slice_fusion.3) | copy-start | bytes 7077892
  120.5 75.3 %copy-start.14 = (bf16[768,1536]{1,0:T(8,128)(2,1)S(1)}, bf16[768,1536]{1,0:T(8,128)(2,1)}, u32[]{:S(2)}) copy-start(bf16[768,1536]{1,0:T(8,128)(2,1)} %copy-done.13) | copy-start | bytes 7077892
  120.5 72.8 %reduce-scatter.5.cloned.1.call-start = ((), (), s32[]{:S(2)}) async-start(), calls=%async_computation.3 | async-start | bytes 1310720 | tf_op jit(solution)/shard_map/reduce_scatter | solution.py:398
  163.7 80.3 %all-gather.7.cloned.1.call-start = ((), (), s32[]{:S(2)}) async-start(), calls=%async_computation.5 | async-start | bytes 1310720 | tf_op jit(solution)/shard_map/all_gather | solution.py:403
  194.3 8.6 %collective-permute-start.5 = (bf16[32,1536]{1,0:T(8,128)(2,1)S(1)}, bf16[32,1536]{1,0:T(8,128)(2,1)S(1)}, u32[]{:S(2)}, u32[]{:S(2)}) collective-permute-start(bf16[32,1536]{1,0:T(8,128)(2,1)S(1)} %dynamic-slice_bitcast_fusion), channel_id=1, source_target_pairs={{0,1},{1,0},{2,3},{3,2},{4,5},{5,4},{6,7},{7,6},{8,9},{9,8},{10,11... | collective-permute-start | bytes 294920 | tf_op jit(solution)/shard_map/ppermute | solution.py:340
  201.9 4.1 %copy-start.2 = (bf16[4,4,32,2,512]{4,3,2,1,0:T(2,128)(2,1)S(1)}, bf16[4,4,32,2,512]{4,3,2,1,0:T(2,128)(2,1)}, u32[]{:S(2)}) copy-start(bf16[4,4,32,2,512]{4,3,2,1,0:T(2,128)(2,1)} %copy-done.1) | copy-start | bytes 3145732
  206.8 20.8 %collective-permute-start.4 = (bf16[384,1024]{1,0:T(8,128)(2,1)}, bf16[384,1024]{1,0:T(8,128)(2,1)S(1)}, u32[]{:S(2)}, u32[]{:S(2)}) collective-permute-start(bf16[384,1024]{1,0:T(8,128)(2,1)} %fusion.8), channel_id=1, source_target_pairs={{0,1},{1,0},{2,3},{3,2},{4,5},{5,4},{6,7},{7,6},{8,9},{9,8},{10,11... | collective-permute-start | bytes 2359304 | tf_op jit(solution)/shard_map/ppermute | solution.py:340
  207.5 20.1 %copy-start.5 = (bf16[1,384,1024]{2,1,0:T(8,128)(2,1)S(1)}, bf16[1,384,1024]{2,1,0:T(8,128)(2,1)}, u32[]{:S(2)}) copy-start(bf16[1,384,1024]{2,1,0:T(8,128)(2,1)} %param.13) | copy-start | bytes 2359300
  207.5 20.1 %copy-start.8 = (f32[2,384,1024]{2,1,0:T(8,128)S(1)}, f32[2,384,1024]{2,1,0:T(8,128)}, u32[]{:S(2)}) copy-start(f32[2,384,1024]{2,1,0:T(8,128)} %fusion.15) | copy-start | bytes 9437188
  208.6 34.2 %copy-start.7 = (bf16[1,384,1024]{2,1,0:T(8,128)(2,1)S(1)}, bf16[1,384,1024]{2,1,0:T(8,128)(2,1)}, u32[]{:S(2)}) copy-start(bf16[1,384,1024]{2,1,0:T(8,128)(2,1)} %param.8) | copy-start | bytes 2359300
  208.6 34.2 %collective-permute-start.3 = (bf16[384,1024]{1,0:T(8,128)(2,1)S(1)}, bf16[384,1024]{1,0:T(8,128)(2,1)S(1)}, u32[]{:S(2)}, u32[]{:S(2)}) collective-permute-start(bf16[384,1024]{1,0:T(8,128)(2,1)S(1)} %fusion.7), channel_id=1, source_target_pairs={{0,1},{1,0},{2,3},{3,2},{4,5},{5,4},{6,7},{7,6},{8,9},{9,8},{10,11... | collective-permute-start | bytes 2359304 | tf_op jit(solution)/shard_map/ppermute | solution.py:340
  (2 other events, 2.4 us)
Sparse Core Ops, SparseCore 0:
  16.7 52.0 all-gather.4
  120.7 43.0 reduce-scatter.2
  166.1 27.1 reduce-scatter.4
  203.8 14.4 all-gather.6

commit v2 on v1

--- a/solution.py
+++ b/solution.py
@@ -394,35 +394,42 @@
     g_qkv = g_qkv.reshape(fsdp_size, ctx_size, dp_size, share, 3 * band).transpose(2, 0, 1, 3, 4)
     g_out = g_out.reshape(fsdp_size, dp_size, share, ctx_size, width // 2).transpose(1, 0, 3, 2, 4)
     partial = jnp.concatenate([g_qkv, g_out], axis=4)
+    out_part = jnp.dot(attended, w_out, preferred_element_type=jnp.float32)
+    tok_part = contract_last(d_qkv, w_qkv)
+    out_part = out_part.reshape(ctx_size, tok_dev, width)
+    tok_part = tok_part.reshape(ctx_size, tok_dev, width)
+
+    def pick(matrix, index):
+        return lax.dynamic_index_in_dim(matrix, index, 0, False)
+
+    out_give = pick(out_part, 1 - me).astype(jnp.bfloat16)
+    tok_give = pick(tok_part, 1 - me).astype(jnp.bfloat16)
     summed = lax.psum_scatter(partial, "dp", scatter_dimension=0, tiled=False)
+    out_sent = other(out_give)
+    tok_sent = other(tok_give)
+    summed, out_sent, tok_sent = lax.optimization_barrier((summed, out_sent, tok_sent))
     summed = lax.psum_scatter(summed, "fsdp", scatter_dimension=0, tiled=False)
     s_qkv = summed[..., : 3 * band]
     kept = lax.dynamic_index_in_dim(s_qkv, me, 0, False)
     sent = lax.dynamic_index_in_dim(s_qkv, 1 - me, 0, False)
     final = jnp.concatenate([ordered(kept, other(sent)), summed[..., 3 * band :]], axis=2)
     final = lax.all_gather(final, "dp", axis=0, tiled=False)
-    f_qkv = final[..., : 3 * band].reshape(dp_size, ctx_size, share, 3, fsdp_size, rows)
-    f_qkv = f_qkv.transpose(3, 0, 2, 4, 1, 5).reshape(3, rows, width).astype(jnp.float32)
+
+    def full_rows(which):
+        block = final[..., which * band : (which + 1) * band]
+        block = block.reshape(dp_size, ctx_size, share, fsdp_size, rows)
+        return block.transpose(0, 2, 3, 1, 4).reshape(rows, width).astype(jnp.float32)
+
     f_out = final[..., 3 * band :].transpose(0, 2, 1, 3).reshape(rows, width).astype(jnp.float32)
 
-    out_part = jnp.dot(attended, w_out, preferred_element_type=jnp.float32)
-    tok_part = contract_last(d_qkv, w_qkv)
-    out_part = out_part.reshape(ctx_size, tok_dev, width)
-    tok_part = tok_part.reshape(ctx_size, tok_dev, width)
-
-    def pick(matrix, index):
-        return lax.dynamic_index_in_dim(matrix, index, 0, False)
-
-    out_sent = other(pick(out_part, 1 - me).astype(jnp.bfloat16))
-    tok_sent = other(pick(tok_part, 1 - me).astype(jnp.bfloat16))
     layer_out = tok_rows.astype(jnp.float32) + pick(out_part, me) + out_sent.astype(jnp.float32)
     grad_tokens = cotangent.astype(jnp.float32) + pick(tok_part, me) + tok_sent.astype(jnp.float32)
     return (
         layer_out.astype(jnp.bfloat16)[None],
         grad_tokens.astype(jnp.bfloat16)[None],
-        f_qkv[0],
-        f_qkv[1],
-        f_qkv[2],
+        full_rows(0),
+        full_rows(1),
+        full_rows(2),
         f_out,
     )
 

time: 261 us -> 232 us (0.89)
  waiting for transfers between devices: 153 us -> 123 us
  other arithmetic: 9.96 us -> 14.5 us
    reduce_scatter x1, waiting for transfers between devices: 43.1 us -> 0.15 us  [striped_device(): summed = lax.psum_scatter(partial, 'dp', scatter_dimension=0, tiled=False)]
    all_gather x1, waiting for transfers between devices: 0.01 us -> 11.6 us  [striped_device(): final = lax.all_gather(final, 'dp', axis=0, tiled=False)]
    squeeze x3 -> x0, local copies, waits for them, and re-layouts: 3.64 us -> none  [the longest x1 1.21 us: striped_device(): f_qkv[2]]
    convert_element_type x3 -> x11, local copies, waits for them, and re-layouts: 3.08 us -> 5.63 us  [the longest x9 5.4 us: full_rows(): block.transpose(0, 2, 3, 1, 4).reshape(rows, width).astype(jnp.float32)]
    unnamed x39 -> x41, local copies, waits for them, and re-layouts: 4.77 us -> 6.15 us
  transfers between devices with their start and end apart: 10 -> 10, of which waited for: 8 -> 10; matrix products, arithmetic and copies ran while one was open for 7% -> 7% of each run, Pallas kernels for 0% -> 0%
where the time goes in v2:
time: 232 us
  waiting for transfers between devices  123 us (53%)
  local copies, waits for them, and re-layouts  27.7 us (12%)
  Pallas kernels  27.5 us (12%)
  matrix products  15.9 us (7%)
  other arithmetic  14.5 us (6%)
  between operations  14.3 us (6%)
  starting transfers between devices  9.09 us (4%)
    ppermute x6, waiting for transfers between devices, other(): return lax.ppermute(matrix, 'ctx', swap)  64.9 us
    reduce_scatter x1, waiting for transfers between devices, striped_device(): summed = lax.psum_scatter(summed, 'fsdp', scatter_dimension=0, tiled=False)  29.5 us
    pallas_call x1, Pallas kernels, attention(): pl.pallas_call(attention_kernel, grid=(band // stripe,), out_shape=[jax.S...  27.5 us
    all_gather x1, waiting for transfers between devices, striped_device(): gathered = lax.all_gather(packed, ('fsdp', 'dp'), axis=0, tiled=False)  16.3 us
    all_gather x1, waiting for transfers between devices, striped_device(): final = lax.all_gather(final, 'dp', axis=0, tiled=False)  11.6 us
    ppermute x6, starting transfers between devices, other(): return lax.ppermute(matrix, 'ctx', swap)  8.93 us
    dot_general x2, matrix products, contract_last(): lax.dot_general(left_rows, right_rows, (((1,), (1,)), ((), ())), preferre...  7.11 us
    unnamed x41, local copies, waits for them, and re-layouts  6.15 us
  transfers between devices with their start and end apart: 10, of which 10 were waited for; matrix products, arithmetic and copies ran while one was open for 7% of the time, Pallas kernels for 0%

profile of v2, /device:TPU:0, one launch (start us, length us, event | category | flops | bytes accessed | tf_op | source)
XLA Modules:
  0.0 231.6 jit_solution(12371297443890003635)
XLA Ops:
  10.7 3.0 %collective-permute-start.1 = (bf16[32,1536]{1,0:T(8,128)(2,1)S(1)}, bf16[32,1536]{1,0:T(8,128)(2,1)S(1)}, u32[]{:S(2)}, u32[]{:S(2)}) collective-permute-start(bf16[32,1536]{1,0:T(8,128)(2,1)S(1)} %reshape.116), channel_id=1, source_target_pairs={{0,1},{1,0},{2,3},{3,2},{4,5},{5,4},{6,7},{7,6},{8,9},{9,8},{10,11... | collective-permute-start | bytes 294920 | tf_op jit(solution)/shard_map/ppermute | solution.py:340
  14.6 1.8 collective-permute-done.1
  17.3 1.9 collective-permute-start.2
  20.2 17.7 %collective-permute-done.2 = bf16[384,1024]{1,0:T(8,128)(2,1)} collective-permute-done((bf16[384,1024]{1,0:T(8,128)(2,1)S(1)}, bf16[384,1024]{1,0:T(8,128)(2,1)}, u32[]{:S(2)}, u32[]{:S(2)}) %collective-permute-start.2) | collective-permute-done | bytes 786464 | tf_op jit(solution)/shard_map/ppermute | solution.py:340
  40.5 12.4 %collective-permute-done = bf16[384,1024]{1,0:T(8,128)(2,1)S(1)} collective-permute-done((bf16[384,1024]{1,0:T(8,128)(2,1)S(1)}, bf16[384,1024]{1,0:T(8,128)(2,1)S(1)}, u32[]{:S(2)}, u32[]{:S(2)}) %collective-permute-start) | collective-permute-done | bytes 786464 | tf_op jit(solution)/shard_map/ppermute | solution.py:340
  53.2 16.3 %all-gather.5.cloned.1.call-done = bf16[32,32,2048]{2,1,0:T(8,128)(2,1)} async-done(((bf16[2,32,2048]{2,1,0:T(8,128)(2,1)}), bf16[32,32,2048]{2,1,0:T(8,128)(2,1)}) %all-gather.5.cloned.1.call-update) | async-done | bytes 4194320 | tf_op jit(solution)/shard_map/all_gather | solution.py:361
  70.8 2.2 slice_bitcast_fusion
  77.8 1.9 convolution_convert_fusion.g_ref
  79.7 27.5 %attention.1 = (bf16[768,512]{1,0:T(8,128)(2,1)S(1)}, bf16[768,512]{1,0:T(8,128)(2,1)S(1)}, bf16[768,512]{1,0:T(8,128)(2,1)S(1)}, bf16[768,512]{1,0:T(8,128)(2,1)S(1)}) custom-call(f32[8,6,768]{2,1,0:T(8,128)S(1)} %copy.82.logs_ref, s32[1,768]{1,0:T(1,128)S(1)} %broadcast_in_dim.23.seg_row_ref, s32[768,1]{1,0:T(8,128)S(1)} %broadcast_in_dim.27.seg_col_ref, ...), custom_call_target="tpu_custom_call" | custom-call | tf_op jit(solution)/shard_map/attention/pallas_call | solution.py:301
  108.5 2.9 %multiply_convert_fusion = bf16[1024,1536]{1,0:T(8,128)(2,1)S(1)} fusion(bf16[768,1024]{1,0:T(8,128)(2,1)S(1)} %bitcast.148, bf16[768,1536]{1,0:T(8,128)(2,1)S(1)} %constant_dynamic-update-slice_fusion.3), kind=kOutput, calls=%fused_computation | convolution fusion | flops 2419064832 | bytes 7077888 | tf_op jit(solution)/shard_map/dot_general | solution.py:22
  111.5 2.1 copy.96
  113.5 2.0 multiply_convert_fusion.1
  115.6 1.8 reshape.123
  117.6 4.5 %pad_maximum_fusion = bf16[4,4,2,32,2048]{4,3,2,1,0:T(8,128)(2,1)} fusion(bf16[4,4,2,32,512]{4,3,2,1,0:T(8,128)(2,1)S(1)} %bitcast.131, bf16[4,4,2,32,1536]{4,3,2,1,0:T(8,128)(2,1)} %bitcast.127), kind=kLoop, calls=%fused_computation.1 | loop fusion | flops 8388608 | bytes 8388608 | tf_op jit(solution)/shard_map/concatenate | solution.py:396
  123.2 5.2 %fusion.14 = f32[2,384,1024]{2,1,0:T(8,128)S(1)} fusion(bf16[2,384,1536]{2,1,0:T(8,128)(2,1)} %bitcast.153, bf16[1024,1536,1]{1,0,2:T(8,128)(2,1)} %bitcast.135), kind=kOutput, calls=%fused_computation.66 | convolution fusion | flops 2415919104 | bytes 8650752 | tf_op jit(solution)/shard_map/dot_general | solution.py:16
  128.5 1.5 collective-permute-start.4
  131.1 1.7 copy-done.2
  133.6 15.4 %collective-permute-done.4 = bf16[384,1024]{1,0:T(8,128)(2,1)S(1)} collective-permute-done((bf16[384,1024]{1,0:T(8,128)(2,1)S(1)}, bf16[384,1024]{1,0:T(8,128)(2,1)S(1)}, u32[]{:S(2)}, u32[]{:S(2)}) %collective-permute-start.4) | collective-permute-done | bytes 786464 | tf_op jit(solution)/shard_map/ppermute | solution.py:340
  149.8 15.3 %collective-permute-done.3 = bf16[384,1024]{1,0:T(8,128)(2,1)S(1)} collective-permute-done((bf16[384,1024]{1,0:T(8,128)(2,1)S(1)}, bf16[384,1024]{1,0:T(8,128)(2,1)S(1)}, u32[]{:S(2)}, u32[]{:S(2)}) %collective-permute-start.3) | collective-permute-done | bytes 786464 | tf_op jit(solution)/shard_map/ppermute | solution.py:340
  165.4 29.5 %reduce-scatter.5.cloned.1.call-done = bf16[1,2,32,2048]{3,2,1,0:T(8,128)(2,1)} async-done(((bf16[4,2,32,2048]{3,2,1,0:T(8,128)(2,1)}), bf16[1,2,32,2048]{3,2,1,0:T(8,128)(2,1)}) %reduce-scatter.5.cloned.1.call-update) | async-done | bytes 262160 | tf_op jit(solution)/shard_map/reduce_scatter | solution.py:411
  195.8 1.5 collective-permute-start.5
  198.2 2.3 collective-permute-done.5
  201.3 3.9 %fusion.9 = (bf16[1,384,1024]{2,1,0:T(8,128)(2,1)}, bf16[1,384,1024]{2,1,0:T(8,128)(2,1)}) fusion(bf16[384,1024]{1,0:T(8,128)(2,1)S(1)} %collective-permute-done.3, f32[2,384,1024]{2,1,0:T(8,128)} %copy-done.2, s32[]{:T(128)S(6)} %select_n.67, bf16[1,384,1024]{2,1,0:T(8,128)(2,1)S(1)} %copy-done.5, bf16[384,1024]{1,0:T(8,128)(2,1)S(1)} %copy-done.13, ...), kind=kLoop, calls=%fused_computation.26 | loop fusion | flops 3932160 | bytes 7864324 | tf_op jit(solution)/shard_map/broadcast_in_dim | solution.py:428
  205.2 11.6 %all-gather.7.cloned.1.call-done = bf16[8,32,2048]{2,1,0:T(8,128)(2,1)} async-done(((bf16[2,32,2048]{2,1,0:T(8,128)(2,1)}), bf16[8,32,2048]{2,1,0:T(8,128)(2,1)}) %all-gather.7.cloned.1.call-update) | async-done | bytes 1048592 | tf_op jit(solution)/shard_map/all_gather | solution.py:416
  (108 shorter events, 31.3 us)
Async XLA Ops:
  7.2 10.1 %copy-start.6 = (bf16[1,384,1024]{2,1,0:T(8,128)(2,1)S(1)}, bf16[1,384,1024]{2,1,0:T(8,128)(2,1)}, u32[]{:S(2)}) copy-start(bf16[1,384,1024]{2,1,0:T(8,128)(2,1)} %param.13) | copy-start | bytes 2359300
  7.2 12.0 %copy-start.4 = (bf16[1,384,1024]{2,1,0:T(8,128)(2,1)S(1)}, bf16[1,384,1024]{2,1,0:T(8,128)(2,1)}, u32[]{:S(2)}) copy-start(bf16[1,384,1024]{2,1,0:T(8,128)(2,1)} %param.8) | copy-start | bytes 2359300
  7.2 12.2 %copy-start.15 = (s32[16,6,8]{0,2,1:T(8,128)S(1)}, s32[16,6,8]{0,2,1:T(8,128)}, u32[]{:S(2)}) copy-start(s32[16,6,8]{0,2,1:T(8,128)} %param.15) | copy-start | bytes 9220
  7.2 12.3 %copy-start.16 = (s32[1,8]{1,0:T(1,128)S(1)}, s32[1,8]{1,0:T(1,128)}, u32[]{:S(2)}) copy-start(s32[1,8]{1,0:T(1,128)} %param.14) | copy-start | bytes 100
  7.2 62.3 %all-gather.5.cloned.1.call-start = ((), (), s32[]{:S(2)}) async-start(), calls=%async_computation.4 | async-start | bytes 4456448 | tf_op jit(solution)/shard_map/all_gather | solution.py:361
  10.7 5.8 %collective-permute-start.1 = (bf16[32,1536]{1,0:T(8,128)(2,1)S(1)}, bf16[32,1536]{1,0:T(8,128)(2,1)S(1)}, u32[]{:S(2)}, u32[]{:S(2)}) collective-permute-start(bf16[32,1536]{1,0:T(8,128)(2,1)S(1)} %reshape.116), channel_id=1, source_target_pairs={{0,1},{1,0},{2,3},{3,2},{4,5},{5,4},{6,7},{7,6},{8,9},{9,8},{10,11... | collective-permute-start | bytes 294920 | tf_op jit(solution)/shard_map/ppermute | solution.py:340
  17.2 148.0 %reduce-scatter.3.cloned.1.call-start = ((), (), s32[]{:S(2)}) async-start(), calls=%async_computation.2 | async-start | bytes 5242880 | tf_op jit(solution)/shard_map/reduce_scatter | solution.py:407
  17.3 20.6 %collective-permute-start.2 = (bf16[384,1024]{1,0:T(8,128)(2,1)S(1)}, bf16[384,1024]{1,0:T(8,128)(2,1)}, u32[]{:S(2)}, u32[]{:S(2)}) collective-permute-start(bf16[384,1024]{1,0:T(8,128)(2,1)S(1)} %bitcast.138), channel_id=1, source_target_pairs={{0,1},{1,0},{2,3},{3,2},{4,5},{5,4},{6,7},{7,6},{8,9},{9,8},{10,11... | collective-permute-start | bytes 2359304 | tf_op jit(solution)/shard_map/ppermute | solution.py:340
  19.2 33.8 %collective-permute-start = (bf16[384,1024]{1,0:T(8,128)(2,1)S(1)}, bf16[384,1024]{1,0:T(8,128)(2,1)S(1)}, u32[]{:S(2)}, u32[]{:S(2)}) collective-permute-start(bf16[384,1024]{1,0:T(8,128)(2,1)S(1)} %bitcast.137), channel_id=1, source_target_pairs={{0,1},{1,0},{2,3},{3,2},{4,5},{5,4},{6,7},{7,6},{8,9},{9,8},{10,11... | collective-permute-start | bytes 2359304 | tf_op jit(solution)/shard_map/ppermute | solution.py:340
  53.2 22.1 %copy-start.10 = (bf16[2,384,1024]{2,1,0:T(8,128)(2,1)}, bf16[2,384,1024]{2,1,0:T(8,128)(2,1)S(1)}, u32[]{:S(2)}) copy-start(bf16[2,384,1024]{2,1,0:T(8,128)(2,1)S(1)} %pad_maximum_fusion.1) | copy-start | bytes 4718596
  73.4 2.0 copy-start.3
  76.4 1.4 copy-start.9
  108.5 2.9 %copy-start.14 = (bf16[768,1536]{1,0:T(8,128)(2,1)}, bf16[768,1536]{1,0:T(8,128)(2,1)S(1)}, u32[]{:S(2)}) copy-start(bf16[768,1536]{1,0:T(8,128)(2,1)S(1)} %constant_dynamic-update-slice_fusion.3) | copy-start | bytes 7077892
  122.1 72.8 %reduce-scatter.5.cloned.1.call-start = ((), (), s32[]{:S(2)}) async-start(), calls=%async_computation.3 | async-start | bytes 1310720 | tf_op jit(solution)/shard_map/reduce_scatter | solution.py:411
  128.4 2.7 %copy-start.8 = (f32[2,384,1024]{2,1,0:T(8,128)}, f32[2,384,1024]{2,1,0:T(8,128)S(1)}, u32[]{:S(2)}) copy-start(f32[2,384,1024]{2,1,0:T(8,128)S(1)} %fusion.14) | copy-start | bytes 9437188
  128.5 20.4 %collective-permute-start.4 = (bf16[384,1024]{1,0:T(8,128)(2,1)S(1)}, bf16[384,1024]{1,0:T(8,128)(2,1)S(1)}, u32[]{:S(2)}, u32[]{:S(2)}) collective-permute-start(bf16[384,1024]{1,0:T(8,128)(2,1)S(1)} %fusion.8), channel_id=1, source_target_pairs={{0,1},{1,0},{2,3},{3,2},{4,5},{5,4},{6,7},{7,6},{8,9},{9,8},{10,11... | collective-permute-start | bytes 2359304 | tf_op jit(solution)/shard_map/ppermute | solution.py:340
  131.1 1.7 copy-start.2
  132.7 68.5 %copy-start.5 = (bf16[1,384,1024]{2,1,0:T(8,128)(2,1)S(1)}, bf16[1,384,1024]{2,1,0:T(8,128)(2,1)}, u32[]{:S(2)}) copy-start(bf16[1,384,1024]{2,1,0:T(8,128)(2,1)} %param.8) | copy-start | bytes 2359300
  132.7 68.6 %copy-start.7 = (bf16[1,384,1024]{2,1,0:T(8,128)(2,1)S(1)}, bf16[1,384,1024]{2,1,0:T(8,128)(2,1)}, u32[]{:S(2)}) copy-start(bf16[1,384,1024]{2,1,0:T(8,128)(2,1)} %param.13) | copy-start | bytes 2359300
  132.9 32.3 %collective-permute-start.3 = (bf16[384,1024]{1,0:T(8,128)(2,1)S(1)}, bf16[384,1024]{1,0:T(8,128)(2,1)S(1)}, u32[]{:S(2)}, u32[]{:S(2)}) collective-permute-start(bf16[384,1024]{1,0:T(8,128)(2,1)S(1)} %fusion.7), channel_id=1, source_target_pairs={{0,1},{1,0},{2,3},{3,2},{4,5},{5,4},{6,7},{7,6},{8,9},{9,8},{10,11... | collective-permute-start | bytes 2359304 | tf_op jit(solution)/shard_map/ppermute | solution.py:340
  165.1 36.2 %copy-start.13 = (bf16[384,1024]{1,0:T(8,128)(2,1)S(1)}, bf16[384,1024]{1,0:T(8,128)(2,1)}, u32[]{:S(2)}) copy-start(bf16[384,1024]{1,0:T(8,128)(2,1)} %copy-done.12) | copy-start | bytes 2359300
  165.3 51.5 %all-gather.7.cloned.1.call-start = ((), (), s32[]{:S(2)}) async-start(), calls=%async_computation.5 | async-start | bytes 1310720 | tf_op jit(solution)/shard_map/all_gather | solution.py:416
  195.8 4.7 %collective-permute-start.5 = (bf16[32,1536]{1,0:T(8,128)(2,1)S(1)}, bf16[32,1536]{1,0:T(8,128)(2,1)S(1)}, u32[]{:S(2)}, u32[]{:S(2)}) collective-permute-start(bf16[32,1536]{1,0:T(8,128)(2,1)S(1)} %dynamic-slice_bitcast_fusion), channel_id=1, source_target_pairs={{0,1},{1,0},{2,3},{3,2},{4,5},{5,4},{6,7},{7,6},{8,9},{9,8},{10,11... | collective-permute-start | bytes 294920 | tf_op jit(solution)/shard_map/ppermute | solution.py:340
  221.9 3.1 %copy-start.1 = (bf16[128,1024]{1,0:T(8,128)(2,1)S(1)}, bf16[128,1024]{1,0:T(8,128)(2,1)}, u32[]{:S(2)}) copy-start(bf16[128,1024]{1,0:T(8,128)(2,1)} %param.9) | copy-start | bytes 786436
  (3 other events, 3.2 us)
Sparse Core Ops, SparseCore 0:
  17.4 52.0 all-gather.4
  122.2 43.0 reduce-scatter.2
  167.7 27.1 reduce-scatter.4
  201.4 15.3 all-gather.6

commit v3 on v2

--- a/solution.py
+++ b/solution.py
@@ -339,6 +339,22 @@
     def other(matrix):
         return lax.ppermute(matrix, "ctx", swap)
 
+    dp_bits, fsdp_bits = dp_size.bit_length() - 1, fsdp_size.bit_length() - 1
+
+    def flip(matrix, axis, size, bit):
+        return lax.ppermute(matrix, axis, [(i, i ^ (1 << bit)) for i in range(size)])
+
+    def join(block, axis, size, bit):
+        peer = flip(block, axis, size, bit)
+        low = (lax.axis_index(axis) >> bit) % 2 == 0
+        return jnp.stack([jnp.where(low, block, peer), jnp.where(low, peer, block)])
+
+    def fold(block, axis, size, bit):
+        side = (lax.axis_index(axis) >> bit) % 2
+        given = flip(lax.dynamic_index_in_dim(block, 1 - side, 0, False), axis, size, bit)
+        kept = lax.dynamic_index_in_dim(block, side, 0, False)
+        return (kept.astype(jnp.float32) + given.astype(jnp.float32)).astype(jnp.bfloat16)
+
     def ordered(own, peer):
         first = me == 0
         return jnp.stack([jnp.where(first, own, peer), jnp.where(first, peer, own)])
@@ -357,22 +373,36 @@
     sent = lax.dynamic_index_in_dim(qkv, 1 - me, 3, False).reshape(share, 3 * band)
     qkv = ordered(kept, other(sent))
     out_share = my_share(w_output).reshape(share, ctx_size, width // 2).transpose(1, 0, 2)
-    packed = jnp.concatenate([qkv, out_share], axis=2)
-    gathered = lax.all_gather(packed, ("fsdp", "dp"), axis=0, tiled=False)
-    gathered = gathered.reshape(fsdp_size, dp_size, ctx_size, share, 3 * band + width // 2)
-    w_qkv = gathered[..., : 3 * band].transpose(0, 2, 1, 3, 4).reshape(width, 3 * band)
-    w_out = gathered[..., 3 * band :].transpose(0, 1, 3, 2, 4).reshape(band, width)
+
+    def spread(block):
+        for bit in reversed(range(fsdp_bits)):
+            block = join(block, "fsdp", fsdp_size, bit)
+        for bit in reversed(range(dp_bits)):
+            block = join(block, "dp", dp_size, bit)
+        block = block.reshape((2,) * (dp_bits + fsdp_bits) + block.shape[-3:])
+        dp_dims = tuple(reversed(range(dp_bits)))
+        fsdp_dims = tuple(dp_bits + d for d in reversed(range(fsdp_bits)))
+        last = dp_bits + fsdp_bits
+        return block, fsdp_dims, dp_dims, last
+
+    qk_block, fsdp_dims, dp_dims, last = spread(qkv[..., : 2 * band])
+    vo_block = spread(jnp.concatenate([qkv[..., 2 * band :], out_share], axis=2))[0]
+    row_order = fsdp_dims + (last,) + dp_dims + (last + 1, last + 2)
+    out_order = fsdp_dims + dp_dims + (last + 1, last, last + 2)
+    w_qk = qk_block.transpose(row_order).reshape(width, 2 * band)
+    w_value_all = vo_block[..., :band].transpose(row_order).reshape(width, band)
+    w_out = vo_block[..., band:].transpose(out_order).reshape(band, width)
 
     tok_all = ordered(tok_rows, tok_peer).reshape(seq_len, width)
     cot_all = ordered(cotangent, cot_peer).reshape(seq_len, width)
     queries = jnp.dot(
-        tok_all, w_qkv[:, :band], preferred_element_type=jnp.float32
+        tok_all, w_qk[:, :band], preferred_element_type=jnp.float32
     ).astype(jnp.bfloat16)
     keys = jnp.dot(
-        tok_all, w_qkv[:, band : 2 * band], preferred_element_type=jnp.float32
+        tok_all, w_qk[:, band:], preferred_element_type=jnp.float32
     ).astype(jnp.bfloat16)
     values = jnp.dot(
-        tok_all, w_qkv[:, 2 * band :], preferred_element_type=jnp.float32
+        tok_all, w_value_all, preferred_element_type=jnp.float32
     ).astype(jnp.bfloat16)
     d_attended = contract_last(cot_all, w_out).astype(jnp.bfloat16)
 
@@ -385,17 +415,40 @@
     attended, d_query, d_key, d_value = attention(
         queries, keys, values, d_attended, logs, segments, rows
     )
-    d_qkv = jnp.concatenate([d_query, d_key, d_value], axis=1)
+    d_qk = jnp.concatenate([d_query, d_key], axis=1)
 
     total_tokens = tok_dev * dp_size * fsdp_size * ctx_size
     grad_scale = total_tokens ** (-0.5)
-    g_qkv = (contract_first(tok_all, d_qkv) * grad_scale).astype(jnp.bfloat16)
-    g_out = (contract_first(attended, cot_all) * grad_scale).astype(jnp.bfloat16)
-    g_qkv = g_qkv.reshape(fsdp_size, ctx_size, dp_size, share, 3 * band).transpose(2, 0, 1, 3, 4)
-    g_out = g_out.reshape(fsdp_size, dp_size, share, ctx_size, width // 2).transpose(1, 0, 3, 2, 4)
-    partial = jnp.concatenate([g_qkv, g_out], axis=4)
+    halves = (2,) * fsdp_bits, (2,) * dp_bits
+
+    def scaled(product):
+        return (product * grad_scale).astype(jnp.bfloat16)
+
+    def row_parts(matrix):
+        columns = matrix.shape[1]
+        parts = matrix.reshape(halves[0] + (ctx_size,) + halves[1] + (share, columns))
+        dp_dims = tuple(fsdp_bits + 1 + d for d in reversed(range(dp_bits)))
+        fsdp_dims = tuple(reversed(range(fsdp_bits)))
+        rest = dp_bits + fsdp_bits + 1
+        return parts.transpose(dp_dims + fsdp_dims + (fsdp_bits, rest, rest + 1))
+
+    g_out = scaled(contract_first(attended, cot_all))
+    out_parts = g_out.reshape(halves[0] + halves[1] + (share, ctx_size, width // 2))
+    rest = dp_bits + fsdp_bits
+    out_parts = out_parts.transpose(
+        tuple(reversed(range(rest)))[:dp_bits]
+        + tuple(reversed(range(fsdp_bits)))
+        + (rest + 1, rest, rest + 2)
+    )
+    vo_sum = jnp.concatenate(
+        [row_parts(scaled(contract_first(tok_all, d_value))), out_parts], axis=-1
+    )
+    qk_sum = row_parts(scaled(contract_first(tok_all, d_qk)))
+    for bit in range(dp_bits):
+        vo_sum = fold(vo_sum, "dp", dp_size, bit)
+        qk_sum = fold(qk_sum, "dp", dp_size, bit)
     out_part = jnp.dot(attended, w_out, preferred_element_type=jnp.float32)
-    tok_part = contract_last(d_qkv, w_qkv)
+    tok_part = contract_last(d_qk, w_qk) + contract_last(d_value, w_value_all)
     out_part = out_part.reshape(ctx_size, tok_dev, width)
     tok_part = tok_part.reshape(ctx_size, tok_dev, width)
 
@@ -404,41 +457,54 @@
 
     out_give = pick(out_part, 1 - me).astype(jnp.bfloat16)
     tok_give = pick(tok_part, 1 - me).astype(jnp.bfloat16)
-    summed = lax.psum_scatter(partial, "dp", scatter_dimension=0, tiled=False)
+    vo_sum, out_give, tok_give = lax.optimization_barrier((vo_sum, out_give, tok_give))
     out_sent = other(out_give)
     tok_sent = other(tok_give)
-    summed, out_sent, tok_sent = lax.optimization_barrier((summed, out_sent, tok_sent))
-    summed = lax.psum_scatter(summed, "fsdp", scatter_dimension=0, tiled=False)
-    s_qkv = summed[..., : 3 * band]
-    kept = lax.dynamic_index_in_dim(s_qkv, me, 0, False)
-    sent = lax.dynamic_index_in_dim(s_qkv, 1 - me, 0, False)
-    final = jnp.concatenate([ordered(kept, other(sent)), summed[..., 3 * band :]], axis=2)
-    final = lax.all_gather(final, "dp", axis=0, tiled=False)
-
-    def full_rows(which):
-        block = final[..., which * band : (which + 1) * band]
+    for bit in range(fsdp_bits):
+        vo_sum = fold(vo_sum, "fsdp", fsdp_size, bit)
+        qk_sum = fold(qk_sum, "fsdp", fsdp_size, bit)
+
+    def over_ctx(matrix):
+        kept = lax.dynamic_index_in_dim(matrix, me, 0, False)
+        sent = lax.dynamic_index_in_dim(matrix, 1 - me, 0, False)
+        return ordered(kept, other(sent))
+
+    def over_dp(block):
+        for bit in reversed(range(dp_bits)):
+            block = join(block, "dp", dp_size, bit)
+        dims = tuple(reversed(range(dp_bits))) + tuple(range(dp_bits, block.ndim))
+        return block.transpose(dims).reshape((dp_size,) + block.shape[dp_bits:])
+
+    vo_final = over_dp(
+        jnp.concatenate([over_ctx(vo_sum[..., :band]), vo_sum[..., band:]], axis=2)
+    )
+    qk_final = over_dp(over_ctx(qk_sum))
+
+    def full_rows(block):
         block = block.reshape(dp_size, ctx_size, share, fsdp_size, rows)
         return block.transpose(0, 2, 3, 1, 4).reshape(rows, width).astype(jnp.float32)
 
-    f_out = final[..., 3 * band :].transpose(0, 2, 1, 3).reshape(rows, width).astype(jnp.float32)
+    f_out = vo_final[..., band:].transpose(0, 2, 1, 3).reshape(rows, width).astype(jnp.float32)
 
     layer_out = tok_rows.astype(jnp.float32) + pick(out_part, me) + out_sent.astype(jnp.float32)
     grad_tokens = cotangent.astype(jnp.float32) + pick(tok_part, me) + tok_sent.astype(jnp.float32)
     return (
         layer_out.astype(jnp.bfloat16)[None],
         grad_tokens.astype(jnp.bfloat16)[None],
-        full_rows(0),
-        full_rows(1),
-        full_rows(2),
+        full_rows(qk_final[..., :band]),
+        full_rows(qk_final[..., band:]),
+        full_rows(vo_final[..., :band]),
         f_out,
     )
 
 
 def per_device(tokens, w_query, w_key, w_value, w_output, grad_out, doc_lengths, block_ids):
     rows = w_query.shape[0]
-    dp_size = lax.axis_size("dp")
+    dp_size, fsdp_size = lax.axis_size("dp"), lax.axis_size("fsdp")
     striped = (
         lax.axis_size("ctx") == 2
+        and dp_size & (dp_size - 1) == 0
+        and fsdp_size & (fsdp_size - 1) == 0
         and rows % 128 == 0
         and rows % HEAD_DIM == 0
         and rows % (dp_size * 16) == 0

time: 232 us -> 192 us (0.83)
  waiting for transfers between devices: 123 us -> 81.3 us
  starting transfers between devices: 9.09 us -> 27.1 us
  between operations: 14.3 us -> 1.61 us
  local copies, waits for them, and re-layouts: 27.7 us -> 24.9 us
    ppermute x0 -> x20, waiting for transfers between devices: none -> 62.6 us  [flip(): return lax.ppermute(matrix, axis, [(i, i ^ 1 << bit) for i in range(size)])]
    ppermute x6 -> x7, waiting for transfers between devices: 64.9 us -> 18.6 us  [other(): return lax.ppermute(matrix, 'ctx', swap)]
    reduce_scatter x2 -> x0, waiting for transfers between devices: 29.7 us -> none  [the longest x1 29.5 us: striped_device(): summed = lax.psum_scatter(summed, 'fsdp', scatter_dimension=0, tiled=False)]
    all_gather x2 -> x0, waiting for transfers between devices: 27.9 us -> none  [the longest x1 16.3 us: striped_device(): gathered = lax.all_gather(packed, ('fsdp', 'dp'), axis=0, tiled=False)]
    ppermute x0 -> x20, starting transfers between devices: none -> 17.2 us  [flip(): return lax.ppermute(matrix, axis, [(i, i ^ 1 << bit) for i in range(size)])]
    concatenate x3 -> x2, other arithmetic: 5.91 us -> 0.03 us  [the longest x1 0.02 us: striped_device(): jnp.concatenate([qkv[..., 2 * band:], out_share], axis=2)]
    another operation x1 -> x22, other arithmetic: 0.18 us -> 4.82 us  [the longest x21 4.64 us: join(): return jnp.stack([jnp.where(low, block, peer), jnp.where(low, peer, block)])]
    transpose x4, local copies, waits for them, and re-layouts: 4.94 us -> 1.38 us  [the longest x1 1.08 us: striped_device(): w_out = vo_block[..., band:].transpose(out_order).reshape(band, width)]
  transfers between devices with their start and end apart: 10 -> 27, of which waited for: 10 -> 13; matrix products, arithmetic and copies ran while one was open for 7% -> 13% of each run, Pallas kernels for 0% -> 0%
where the time goes in v3:
time: 192 us; the launch traced here: 191 us
  waiting for transfers between devices  81.3 us (42%)
  Pallas kernels  27.5 us (14%)
  starting transfers between devices  27.1 us (14%)
  local copies, waits for them, and re-layouts  24.9 us (13%)
  matrix products  14.4 us (8%)
  other arithmetic  13.7 us (7%)
    ppermute x20, waiting for transfers between devices, flip(): return lax.ppermute(matrix, axis, [(i, i ^ 1 << bit) for i in range(size)])  62.6 us
    pallas_call x1, Pallas kernels, attention(): pl.pallas_call(attention_kernel, grid=(band // stripe,), out_shape=[jax.S...  27.5 us
    ppermute x7, waiting for transfers between devices, other(): return lax.ppermute(matrix, 'ctx', swap)  18.6 us
    ppermute x20, starting transfers between devices, flip(): return lax.ppermute(matrix, axis, [(i, i ^ 1 << bit) for i in range(size)])  17.2 us
    ppermute x7, starting transfers between devices, other(): return lax.ppermute(matrix, 'ctx', swap)  9.95 us
    unnamed x46, local copies, waits for them, and re-layouts  5.8 us
    convert_element_type x9, local copies, waits for them, and re-layouts, full_rows(): block.transpose(0, 2, 3, 1, 4).reshape(rows, width).astype(jnp.float32)  5.4 us
    dot_general x3, matrix products, contract_first(): lax.dot_general(left_rows, right_rows, (((0,), (0,)), ((), ())), preferre...  4.84 us
  transfers between devices with their start and end apart: 27, of which 13 were waited for; matrix products, arithmetic and copies ran while one was open for 13% of the time, Pallas kernels for 0%

profile of v3, /device:TPU:0, one launch (start us, length us, event | category | flops | bytes accessed | tf_op | source)
XLA Modules:
  0.0 190.5 jit_solution(5892539822425388705)
XLA Ops:
  3.4 3.0 %collective-permute-start.1 = (bf16[32,1536]{1,0:T(8,128)(2,1)S(1)}, bf16[32,1536]{1,0:T(8,128)(2,1)S(1)}, u32[]{:S(2)}, u32[]{:S(2)}) collective-permute-start(bf16[32,1536]{1,0:T(8,128)(2,1)S(1)} %reshape.142), channel_id=1, source_target_pairs={{0,1},{1,0},{2,3},{3,2},{4,5},{5,4},{6,7},{7,6},{8,9},{9,8},{10,11... | collective-permute-start | bytes 294920 | tf_op jit(solution)/shard_map/ppermute | solution.py:340
  6.5 1.9 %collective-permute-start = (bf16[384,1024]{1,0:T(8,128)(2,1)S(1)}, bf16[384,1024]{1,0:T(8,128)(2,1)}, u32[]{:S(2)}, u32[]{:S(2)}) collective-permute-start(bf16[384,1024]{1,0:T(8,128)(2,1)S(1)} %bitcast.257), channel_id=1, source_target_pairs={{0,1},{1,0},{2,3},{3,2},{4,5},{5,4},{6,7},{7,6},{8,9},{9,8},{10,11... | collective-permute-start | bytes 2359304 | tf_op jit(solution)/shard_map/ppermute | solution.py:340
  10.0 3.2 %collective-permute-start.2 = (bf16[2,32,1024]{2,1,0:T(8,128)(2,1)S(1)}, bf16[2,32,1024]{2,1,0:T(8,128)(2,1)S(1)}, u32[]{:S(2)}, u32[]{:S(2)}) collective-permute-start(bf16[2,32,1024]{2,1,0:T(8,128)(2,1)S(1)} %get-tuple-element.57), channel_id=1, source_target_pairs={{0,4},{2,6},{4,0},{6,2},{1,5},{3,7},{5,1},{7,3},{8,12},{10,14},{12... | collective-permute-start | bytes 393224 | tf_op jit(solution)/shard_map/ppermute | solution.py:345
  13.3 8.5 %collective-permute-done.2 = bf16[2,32,1024]{2,1,0:T(8,128)(2,1)S(1)} collective-permute-done((bf16[2,32,1024]{2,1,0:T(8,128)(2,1)S(1)}, bf16[2,32,1024]{2,1,0:T(8,128)(2,1)S(1)}, u32[]{:S(2)}, u32[]{:S(2)}) %collective-permute-start.2) | collective-permute-done | bytes 131104 | tf_op jit(solution)/shard_map/ppermute | solution.py:345
  24.7 6.5 %collective-permute-done.3 = bf16[2,2,32,1024]{3,2,1,0:T(8,128)(2,1)S(1)} collective-permute-done((bf16[2,2,32,1024]{3,2,1,0:T(8,128)(2,1)S(1)}, bf16[2,2,32,1024]{3,2,1,0:T(8,128)(2,1)S(1)}, u32[]{:S(2)}, u32[]{:S(2)}) %collective-permute-start.3) | collective-permute-done | bytes 262176 | tf_op jit(solution)/shard_map/ppermute | solution.py:345
  34.7 1.6 copy.64.logs_ref
  38.1 9.1 %collective-permute-done.4 = bf16[2,2,2,32,1024]{4,3,2,1,0:T(8,128)(2,1)} collective-permute-done((bf16[2,2,2,32,1024]{4,3,2,1,0:T(8,128)(2,1)}, bf16[2,2,2,32,1024]{4,3,2,1,0:T(8,128)(2,1)}, u32[]{:S(2)}, u32[]{:S(2)}) %collective-permute-start.4) | collective-permute-done | bytes 524320 | tf_op jit(solution)/shard_map/ppermute | solution.py:345
  51.4 1.6 collective-permute-done.8
  55.2 1.9 convolution_convert_fusion.3.q_ref
  59.5 1.7 reshape.169
  64.4 1.9 %convolution_convert_fusion.g_ref = bf16[768,512]{1,0:T(8,128)(2,1)} fusion(bf16[768,1024]{1,0:T(8,128)(2,1)S(1)} %bitcast.275, bf16[512,1024]{1,0:T(8,128)(2,1)S(1)} %bitcast.278), kind=kOutput, calls=%fused_computation.25 | convolution fusion | flops 805699584 | bytes 3407872 | tf_op jit(solution)/shard_map/dot_general | solution.py:16
  66.3 27.5 %attention.1 = (bf16[768,512]{1,0:T(8,128)(2,1)S(1)}, bf16[768,512]{1,0:T(8,128)(2,1)S(1)}, bf16[768,512]{1,0:T(8,128)(2,1)S(1)}, bf16[768,512]{1,0:T(8,128)(2,1)S(1)}) custom-call(f32[8,6,768]{2,1,0:T(8,128)S(1)} %copy-done.1, s32[1,768]{1,0:T(1,128)S(1)} %broadcast_in_dim.23.seg_row_ref, s32[768,1]{1,0:T(8,128)S(1)} %broadcast_in_dim.27.seg_col_ref, ...), custom_call_target="tpu_custom_call" | custom-call | tf_op jit(solution)/shard_map/attention/pallas_call | solution.py:301
  94.7 2.0 %multiply_convert_fusion.1 = bf16[512,1024]{1,0:T(8,128)(2,1)} fusion(bf16[768,512]{1,0:T(8,128)(2,1)S(1)} %get-tuple-element.13, bf16[768,1024]{1,0:T(8,128)(2,1)S(1)} %bitcast.276), kind=kOutput, calls=%fused_computation.12 | convolution fusion | flops 806354944 | bytes 3407872 | tf_op jit(solution)/shard_map/dot_general | solution.py:22
  96.7 2.7 %reshape.149 = bf16[2,2,2,2,32,2,512]{6,5,4,3,2,1,0:T(2,128)(2,1)} reshape(bf16[512,1024]{1,0:T(8,128)(2,1)} %multiply_convert_fusion.1) | data formatting | bytes 2097152 | tf_op jit(solution)/shard_map/reshape | solution.py:436
  99.3 1.6 copy.82
  102.4 1.9 multiply_convert_fusion
  106.1 1.8 fusion.33
  113.5 11.9 %collective-permute-done.12 = bf16[2,2,2,32,1024]{4,3,2,1,0:T(8,128)(2,1)S(1)} collective-permute-done((bf16[2,2,2,32,1024]{4,3,2,1,0:T(8,128)(2,1)S(1)}, bf16[2,2,2,32,1024]{4,3,2,1,0:T(8,128)(2,1)S(1)}, u32[]{:S(2)}, u32[]{:S(2)}) %collective-permute-start.12) | collective-permute-done | bytes 524320 | tf_op jit(solution)/shard_map/ppermute | solution.py:345
  125.7 10.5 %collective-permute-done.16 = bf16[2,2,2,32,1024]{4,3,2,0,1:T(8,128)(2,1)S(1)} collective-permute-done((bf16[2,2,2,32,1024]{4,3,2,0,1:T(8,128)(2,1)S(1)}, bf16[2,2,2,32,1024]{4,3,2,0,1:T(8,128)(2,1)S(1)}, u32[]{:S(2)}, u32[]{:S(2)}) %collective-permute-start.16) | collective-permute-done | bytes 524320 | tf_op jit(solution)/shard_map/ppermute | solution.py:345
  138.8 4.6 %collective-permute-start.23 = (bf16[2,32,1024]{2,1,0:T(8,128)(2,1)S(1)}, bf16[2,32,1024]{2,1,0:T(8,128)(2,1)S(1)}, u32[]{:S(2)}, u32[]{:S(2)}) collective-permute-start(bf16[2,32,1024]{2,1,0:T(8,128)(2,1)S(1)} %dynamic-slice_bitcast_fusion.5), channel_id=1, source_target_pairs={{0,4},{2,6},{4,0},{6,2},{1,5},{3,7},{5,1},{7,3},{8,12},{10,14},{12... | collective-permute-start | bytes 393224 | tf_op jit(solution)/shard_map/ppermute | solution.py:345
  143.3 4.0 %collective-permute-done.17 = bf16[2,2,32,1024]{3,2,1,0:T(8,128)(2,1)S(1)} collective-permute-done((bf16[2,2,32,1024]{3,2,1,0:T(8,128)(2,1)S(1)}, bf16[2,2,32,1024]{3,2,1,0:T(8,128)(2,1)S(1)}, u32[]{:S(2)}, u32[]{:S(2)}) %collective-permute-start.17) | collective-permute-done | bytes 262176 | tf_op jit(solution)/shard_map/ppermute | solution.py:345
  150.2 5.0 %collective-permute-done.18 = bf16[2,32,1024]{2,1,0:T(8,128)(2,1)S(1)} collective-permute-done((bf16[2,32,1024]{2,1,0:T(8,128)(2,1)S(1)}, bf16[2,32,1024]{2,1,0:T(8,128)(2,1)S(1)}, u32[]{:S(2)}, u32[]{:S(2)}) %collective-permute-start.18) | collective-permute-done | bytes 131104 | tf_op jit(solution)/shard_map/ppermute | solution.py:345
  156.5 17.5 %collective-permute-done.24 = bf16[32,512]{1,0:T(8,128)(2,1)S(1)} collective-permute-done((bf16[32,512]{1,0:T(8,128)(2,1)S(1)}, bf16[32,512]{1,0:T(8,128)(2,1)S(1)}, u32[]{:S(2)}, u32[]{:S(2)}) %collective-permute-start.24) | collective-permute-done | bytes 32800 | tf_op jit(solution)/shard_map/ppermute | solution.py:340
  176.3 2.8 %collective-permute-done.25 = bf16[2,32,1024]{2,1,0:T(8,128)(2,1)S(1)} collective-permute-done((bf16[2,32,1024]{2,1,0:T(8,128)(2,1)S(1)}, bf16[2,32,1024]{2,1,0:T(8,128)(2,1)S(1)}, u32[]{:S(2)}, u32[]{:S(2)}) %collective-permute-start.25) | collective-permute-done | bytes 131104 | tf_op jit(solution)/shard_map/ppermute | solution.py:345
  (185 shorter events, 54.2 us)
Async XLA Ops:
  3.4 6.5 %collective-permute-start.1 = (bf16[32,1536]{1,0:T(8,128)(2,1)S(1)}, bf16[32,1536]{1,0:T(8,128)(2,1)S(1)}, u32[]{:S(2)}, u32[]{:S(2)}) collective-permute-start(bf16[32,1536]{1,0:T(8,128)(2,1)S(1)} %reshape.142), channel_id=1, source_target_pairs={{0,1},{1,0},{2,3},{3,2},{4,5},{5,4},{6,7},{7,6},{8,9},{9,8},{10,11... | collective-permute-start | bytes 294920 | tf_op jit(solution)/shard_map/ppermute | solution.py:340
  6.4 42.1 %collective-permute-start.10 = (bf16[384,1024]{1,0:T(8,128)(2,1)S(1)}, bf16[384,1024]{1,0:T(8,128)(2,1)S(1)}, u32[]{:S(2)}, u32[]{:S(2)}) collective-permute-start(bf16[384,1024]{1,0:T(8,128)(2,1)S(1)} %bitcast.258), channel_id=1, source_target_pairs={{0,1},{1,0},{2,3},{3,2},{4,5},{5,4},{6,7},{7,6},{8,9},{9,8},{10,11... | collective-permute-start | bytes 2359304 | tf_op jit(solution)/shard_map/ppermute | solution.py:340
  6.5 42.1 %collective-permute-start = (bf16[384,1024]{1,0:T(8,128)(2,1)S(1)}, bf16[384,1024]{1,0:T(8,128)(2,1)}, u32[]{:S(2)}, u32[]{:S(2)}) collective-permute-start(bf16[384,1024]{1,0:T(8,128)(2,1)S(1)} %bitcast.257), channel_id=1, source_target_pairs={{0,1},{1,0},{2,3},{3,2},{4,5},{5,4},{6,7},{7,6},{8,9},{9,8},{10,11... | collective-permute-start | bytes 2359304 | tf_op jit(solution)/shard_map/ppermute | solution.py:340
  10.0 11.9 %collective-permute-start.2 = (bf16[2,32,1024]{2,1,0:T(8,128)(2,1)S(1)}, bf16[2,32,1024]{2,1,0:T(8,128)(2,1)S(1)}, u32[]{:S(2)}, u32[]{:S(2)}) collective-permute-start(bf16[2,32,1024]{2,1,0:T(8,128)(2,1)S(1)} %get-tuple-element.57), channel_id=1, source_target_pairs={{0,4},{2,6},{4,0},{6,2},{1,5},{3,7},{5,1},{7,3},{8,12},{10,14},{12... | collective-permute-start | bytes 393224 | tf_op jit(solution)/shard_map/ppermute | solution.py:345
  13.2 10.3 %collective-permute-start.6 = (bf16[2,32,1024]{2,1,0:T(8,128)(2,1)S(1)}, bf16[2,32,1024]{2,1,0:T(8,128)(2,1)S(1)}, u32[]{:S(2)}, u32[]{:S(2)}) collective-permute-start(bf16[2,32,1024]{2,1,0:T(8,128)(2,1)S(1)} %get-tuple-element.56), channel_id=1, source_target_pairs={{0,4},{2,6},{4,0},{6,2},{1,5},{3,7},{5,1},{7,3},{8,12},{10,14},{12... | collective-permute-start | bytes 393224 | tf_op jit(solution)/shard_map/ppermute | solution.py:345
  21.9 9.3 %collective-permute-start.3 = (bf16[2,2,32,1024]{3,2,1,0:T(8,128)(2,1)S(1)}, bf16[2,2,32,1024]{3,2,1,0:T(8,128)(2,1)S(1)}, u32[]{:S(2)}, u32[]{:S(2)}) collective-permute-start(bf16[2,2,32,1024]{3,2,1,0:T(8,128)(2,1)S(1)} %pad_maximum_fusion.8), channel_id=1, source_target_pairs={{0,2},{2,0},{4,6},{6,4},{1,3},{3,1},{5,7},{7,5},{8,10},{10,8},{12,... | collective-permute-start | bytes 786440 | tf_op jit(solution)/shard_map/ppermute | solution.py:345
  24.2 12.1 %collective-permute-start.7 = (bf16[2,2,32,1024]{3,2,1,0:T(8,128)(2,1)}, bf16[2,2,32,1024]{3,2,1,0:T(8,128)(2,1)}, u32[]{:S(2)}, u32[]{:S(2)}) collective-permute-start(bf16[2,2,32,1024]{3,2,1,0:T(8,128)(2,1)} %pad_maximum_fusion.9), channel_id=1, source_target_pairs={{0,2},{2,0},{4,6},{6,4},{1,3},{3,1},{5,7},{7,5},{8,10},{10,8},{12,... | collective-permute-start | bytes 786440 | tf_op jit(solution)/shard_map/ppermute | solution.py:345
  32.1 15.2 %collective-permute-start.4 = (bf16[2,2,2,32,1024]{4,3,2,1,0:T(8,128)(2,1)}, bf16[2,2,2,32,1024]{4,3,2,1,0:T(8,128)(2,1)}, u32[]{:S(2)}, u32[]{:S(2)}) collective-permute-start(bf16[2,2,2,32,1024]{4,3,2,1,0:T(8,128)(2,1)} %pad_maximum_fusion.5), channel_id=1, source_target_pairs={{0,16},{8,24},{16,0},{24,8},{1,17},{9,25},{17,1},{25,9},{2,18},{10... | collective-permute-start | bytes 1572872 | tf_op jit(solution)/shard_map/ppermute | solution.py:345
  37.4 15.6 %collective-permute-start.8 = (bf16[2,2,2,32,1024]{4,3,2,1,0:T(8,128)(2,1)S(1)}, bf16[2,2,2,32,1024]{4,3,2,1,0:T(8,128)(2,1)S(1)}, u32[]{:S(2)}, u32[]{:S(2)}) collective-permute-start(bf16[2,2,2,32,1024]{4,3,2,1,0:T(8,128)(2,1)S(1)} %pad_maximum_fusion.6), channel_id=1, source_target_pairs={{0,16},{8,24},{16,0},{24,8},{1,17},{9,25},{17,1},{25,9},{2,18},{10... | collective-permute-start | bytes 1572872 | tf_op jit(solution)/shard_map/ppermute | solution.py:345
  104.5 7.2 %collective-permute-start.15 = (bf16[2,2,2,2,32,1024]{5,4,0,3,1,2:T(8,128)(2,1)S(1)}, bf16[2,2,2,2,32,1024]{5,4,0,3,1,2:T(8,128)(2,1)S(1)}, u32[]{:S(2)}, u32[]{:S(2)}) collective-permute-start(bf16[2,2,2,2,32,1024]{5,4,0,3,1,2:T(8,128)(2,1)S(1)} %dynamic-slice_bitcast_fusion), channel_id=1, source_target_pairs={{0,8},{8,0},{16,24},{24,16},{1,9},{9,1},{17,25},{25,17},{2,10},{10... | collective-permute-start | bytes 3145736 | tf_op jit(solution)/shard_map/ppermute | solution.py:345
  105.2 5.0 %collective-permute-start.11 = (bf16[2,2,2,2,32,1024]{5,4,3,2,1,0:T(8,128)(2,1)S(1)}, bf16[2,2,2,2,32,1024]{5,4,3,2,1,0:T(8,128)(2,1)S(1)}, u32[]{:S(2)}, u32[]{:S(2)}) collective-permute-start(bf16[2,2,2,2,32,1024]{5,4,3,2,1,0:T(8,128)(2,1)S(1)} %fusion.9), channel_id=1, source_target_pairs={{0,8},{8,0},{16,24},{24,16},{1,9},{9,1},{17,25},{25,17},{2,10},{10... | collective-permute-start | bytes 3145736 | tf_op jit(solution)/shard_map/ppermute | solution.py:345
  110.6 14.8 %collective-permute-start.12 = (bf16[2,2,2,32,1024]{4,3,2,1,0:T(8,128)(2,1)S(1)}, bf16[2,2,2,32,1024]{4,3,2,1,0:T(8,128)(2,1)S(1)}, u32[]{:S(2)}, u32[]{:S(2)}) collective-permute-start(bf16[2,2,2,32,1024]{4,3,2,1,0:T(8,128)(2,1)S(1)} %dynamic-slice_bitcast_fusion.2), channel_id=1, source_target_pairs={{0,16},{8,24},{16,0},{24,8},{1,17},{9,25},{17,1},{25,9},{2,18},{10... | collective-permute-start | bytes 1572872 | tf_op jit(solution)/shard_map/ppermute | solution.py:345
  112.2 24.0 %collective-permute-start.16 = (bf16[2,2,2,32,1024]{4,3,2,0,1:T(8,128)(2,1)S(1)}, bf16[2,2,2,32,1024]{4,3,2,0,1:T(8,128)(2,1)S(1)}, u32[]{:S(2)}, u32[]{:S(2)}) collective-permute-start(bf16[2,2,2,32,1024]{4,3,2,0,1:T(8,128)(2,1)S(1)} %dynamic-slice_bitcast_fusion.1), channel_id=1, source_target_pairs={{0,16},{8,24},{16,0},{24,8},{1,17},{9,25},{17,1},{25,9},{2,18},{10... | collective-permute-start | bytes 1572872 | tf_op jit(solution)/shard_map/ppermute | solution.py:345
  125.7 13.0 %collective-permute-start.22 = (bf16[2,2,32,1024]{3,2,1,0:T(8,128)(2,1)S(1)}, bf16[2,2,32,1024]{3,2,1,0:T(8,128)(2,1)S(1)}, u32[]{:S(2)}, u32[]{:S(2)}) collective-permute-start(bf16[2,2,32,1024]{3,2,1,0:T(8,128)(2,1)S(1)} %dynamic-slice_bitcast_fusion.3), channel_id=1, source_target_pairs={{0,2},{2,0},{4,6},{6,4},{1,3},{3,1},{5,7},{7,5},{8,10},{10,8},{12,... | collective-permute-start | bytes 786440 | tf_op jit(solution)/shard_map/ppermute | solution.py:345
  136.5 10.8 %collective-permute-start.17 = (bf16[2,2,32,1024]{3,2,1,0:T(8,128)(2,1)S(1)}, bf16[2,2,32,1024]{3,2,1,0:T(8,128)(2,1)S(1)}, u32[]{:S(2)}, u32[]{:S(2)}) collective-permute-start(bf16[2,2,32,1024]{3,2,1,0:T(8,128)(2,1)S(1)} %dynamic-slice_bitcast_fusion.4), channel_id=1, source_target_pairs={{0,2},{2,0},{4,6},{6,4},{1,3},{3,1},{5,7},{7,5},{8,10},{10,8},{12,... | collective-permute-start | bytes 786440 | tf_op jit(solution)/shard_map/ppermute | solution.py:345
  136.6 44.1 %collective-permute-start.13 = (bf16[384,1024]{1,0:T(8,128)(2,1)S(1)}, bf16[384,1024]{1,0:T(8,128)(2,1)S(1)}, u32[]{:S(2)}, u32[]{:S(2)}) collective-permute-start(bf16[384,1024]{1,0:T(8,128)(2,1)S(1)} %fusion.17), channel_id=1, source_target_pairs={{0,1},{1,0},{2,3},{3,2},{4,5},{5,4},{6,7},{7,6},{8,9},{9,8},{10,11... | collective-permute-start | bytes 2359304 | tf_op jit(solution)/shard_map/ppermute | solution.py:340
  137.8 44.2 %collective-permute-start.14 = (bf16[384,1024]{1,0:T(8,128)(2,1)S(1)}, bf16[384,1024]{1,0:T(8,128)(2,1)S(1)}, u32[]{:S(2)}, u32[]{:S(2)}) collective-permute-start(bf16[384,1024]{1,0:T(8,128)(2,1)S(1)} %fusion.18), channel_id=1, source_target_pairs={{0,1},{1,0},{2,3},{3,2},{4,5},{5,4},{6,7},{7,6},{8,9},{9,8},{10,11... | collective-permute-start | bytes 2359304 | tf_op jit(solution)/shard_map/ppermute | solution.py:340
  138.8 9.9 %collective-permute-start.23 = (bf16[2,32,1024]{2,1,0:T(8,128)(2,1)S(1)}, bf16[2,32,1024]{2,1,0:T(8,128)(2,1)S(1)}, u32[]{:S(2)}, u32[]{:S(2)}) collective-permute-start(bf16[2,32,1024]{2,1,0:T(8,128)(2,1)S(1)} %dynamic-slice_bitcast_fusion.5), channel_id=1, source_target_pairs={{0,4},{2,6},{4,0},{6,2},{1,5},{3,7},{5,1},{7,3},{8,12},{10,14},{12... | collective-permute-start | bytes 393224 | tf_op jit(solution)/shard_map/ppermute | solution.py:345
  147.4 7.8 %collective-permute-start.18 = (bf16[2,32,1024]{2,1,0:T(8,128)(2,1)S(1)}, bf16[2,32,1024]{2,1,0:T(8,128)(2,1)S(1)}, u32[]{:S(2)}, u32[]{:S(2)}) collective-permute-start(bf16[2,32,1024]{2,1,0:T(8,128)(2,1)S(1)} %dynamic-slice_bitcast_fusion.6), channel_id=1, source_target_pairs={{0,4},{2,6},{4,0},{6,2},{1,5},{3,7},{5,1},{7,3},{8,12},{10,14},{12... | collective-permute-start | bytes 393224 | tf_op jit(solution)/shard_map/ppermute | solution.py:345
  148.7 25.3 %collective-permute-start.24 = (bf16[32,512]{1,0:T(8,128)(2,1)S(1)}, bf16[32,512]{1,0:T(8,128)(2,1)S(1)}, u32[]{:S(2)}, u32[]{:S(2)}) collective-permute-start(bf16[32,512]{1,0:T(8,128)(2,1)S(1)} %dynamic-slice_bitcast_fusion.8), channel_id=1, source_target_pairs={{0,1},{1,0},{2,3},{3,2},{4,5},{5,4},{6,7},{7,6},{8,9},{9,8},{10,11... | collective-permute-start | bytes 98312 | tf_op jit(solution)/shard_map/ppermute | solution.py:340
  155.2 20.1 %collective-permute-start.19 = (bf16[32,1024]{1,0:T(8,128)(2,1)S(1)}, bf16[32,1024]{1,0:T(8,128)(2,1)S(1)}, u32[]{:S(2)}, u32[]{:S(2)}) collective-permute-start(bf16[32,1024]{1,0:T(8,128)(2,1)S(1)} %dynamic-slice_bitcast_fusion.7), channel_id=1, source_target_pairs={{0,1},{1,0},{2,3},{3,2},{4,5},{5,4},{6,7},{7,6},{8,9},{9,8},{10,11... | collective-permute-start | bytes 196616 | tf_op jit(solution)/shard_map/ppermute | solution.py:340
  174.1 5.0 %collective-permute-start.25 = (bf16[2,32,1024]{2,1,0:T(8,128)(2,1)S(1)}, bf16[2,32,1024]{2,1,0:T(8,128)(2,1)S(1)}, u32[]{:S(2)}, u32[]{:S(2)}) collective-permute-start(bf16[2,32,1024]{2,1,0:T(8,128)(2,1)S(1)} %pad_maximum_fusion.14), channel_id=1, source_target_pairs={{0,16},{8,24},{16,0},{24,8},{1,17},{9,25},{17,1},{25,9},{2,18},{10... | collective-permute-start | bytes 393224 | tf_op jit(solution)/shard_map/ppermute | solution.py:345
  175.3 5.2 %collective-permute-start.20 = (bf16[2,32,1024]{2,1,0:T(8,128)(2,1)S(1)}, bf16[2,32,1024]{2,1,0:T(8,128)(2,1)S(1)}, u32[]{:S(2)}, u32[]{:S(2)}) collective-permute-start(bf16[2,32,1024]{2,1,0:T(8,128)(2,1)S(1)} %pad_maximum_fusion.13), channel_id=1, source_target_pairs={{0,16},{8,24},{16,0},{24,8},{1,17},{9,25},{17,1},{25,9},{2,18},{10... | collective-permute-start | bytes 393224 | tf_op jit(solution)/shard_map/ppermute | solution.py:345
  180.6 6.1 %collective-permute-start.21 = (bf16[2,2,32,1024]{3,2,1,0:T(8,128)(2,1)S(1)}, bf16[2,2,32,1024]{3,2,1,0:T(8,128)(2,1)S(1)}, u32[]{:S(2)}, u32[]{:S(2)}) collective-permute-start(bf16[2,2,32,1024]{3,2,1,0:T(8,128)(2,1)S(1)} %pad_maximum_fusion.10), channel_id=1, source_target_pairs={{0,8},{8,0},{16,24},{24,16},{1,9},{9,1},{17,25},{25,17},{2,10},{10... | collective-permute-start | bytes 786440 | tf_op jit(solution)/shard_map/ppermute | solution.py:345
  (23 other events, 112.5 us)

commit v4 on v3

--- a/solution.py
+++ b/solution.py
@@ -457,12 +457,14 @@
 
     out_give = pick(out_part, 1 - me).astype(jnp.bfloat16)
     tok_give = pick(tok_part, 1 - me).astype(jnp.bfloat16)
-    vo_sum, out_give, tok_give = lax.optimization_barrier((vo_sum, out_give, tok_give))
     out_sent = other(out_give)
     tok_sent = other(tok_give)
+    qk_sum, out_sent = lax.optimization_barrier((qk_sum, out_sent))
     for bit in range(fsdp_bits):
         vo_sum = fold(vo_sum, "fsdp", fsdp_size, bit)
         qk_sum = fold(qk_sum, "fsdp", fsdp_size, bit)
+        if bit == 0:
+            qk_sum, tok_sent = lax.optimization_barrier((qk_sum, tok_sent))
 
     def over_ctx(matrix):
         kept = lax.dynamic_index_in_dim(matrix, me, 0, False)

time: 192 us -> 169 us (0.88)
  waiting for transfers between devices: 81.3 us -> 59.5 us
  starting transfers between devices: 27.1 us -> 30.4 us
    ppermute x7, waiting for transfers between devices: 18.6 us -> 2.84 us  [other(): return lax.ppermute(matrix, 'ctx', swap)]
    ppermute x20, waiting for transfers between devices: 62.6 us -> 56.6 us  [flip(): return lax.ppermute(matrix, axis, [(i, i ^ 1 << bit) for i in range(size)])]
    ppermute x20, starting transfers between devices: 17.2 us -> 21.1 us  [flip(): return lax.ppermute(matrix, axis, [(i, i ^ 1 << bit) for i in range(size)])]
    unnamed x46 -> x44, local copies, waits for them, and re-layouts: 5.8 us -> 5.52 us
  transfers between devices with their start and end apart: 27 -> 27, of which waited for: 13 -> 14; matrix products, arithmetic and copies ran while one was open for 13% -> 15% of each run, Pallas kernels for 0% -> 0%
where the time goes in v4:
time: 169 us
  waiting for transfers between devices  59.5 us (35%)
  starting transfers between devices  30.4 us (18%)
  Pallas kernels  27.4 us (16%)
  local copies, waits for them, and re-layouts  23.1 us (14%)
  matrix products  14.4 us (9%)
  other arithmetic  12.1 us (7%)
    ppermute x20, waiting for transfers between devices, flip(): return lax.ppermute(matrix, axis, [(i, i ^ 1 << bit) for i in range(size)])  56.6 us
    pallas_call x1, Pallas kernels, attention(): pl.pallas_call(attention_kernel, grid=(band // stripe,), out_shape=[jax.S...  27.4 us
    ppermute x20, starting transfers between devices, flip(): return lax.ppermute(matrix, axis, [(i, i ^ 1 << bit) for i in range(size)])  21.1 us
    ppermute x7, starting transfers between devices, other(): return lax.ppermute(matrix, 'ctx', swap)  9.3 us
    unnamed x44, local copies, waits for them, and re-layouts  5.52 us
    convert_element_type x9, local copies, waits for them, and re-layouts, full_rows(): block.transpose(0, 2, 3, 1, 4).reshape(rows, width).astype(jnp.float32)  5.4 us
    dot_general x3, matrix products, contract_first(): lax.dot_general(left_rows, right_rows, (((0,), (0,)), ((), ())), preferre...  4.86 us
    dot_general x3, matrix products, contract_last(): lax.dot_general(left_rows, right_rows, (((1,), (1,)), ((), ())), preferre...  4.73 us
  transfers between devices with their start and end apart: 27, of which 14 were waited for; matrix products, arithmetic and copies ran while one was open for 15% of the time, Pallas kernels for 0%

profile of v4, /device:TPU:0, one launch (start us, length us, event | category | flops | bytes accessed | tf_op | source)
XLA Modules:
  0.0 168.5 jit_solution(3885767885868656214)
XLA Ops:
  3.4 3.0 %collective-permute-start.1 = (bf16[32,1536]{1,0:T(8,128)(2,1)S(1)}, bf16[32,1536]{1,0:T(8,128)(2,1)S(1)}, u32[]{:S(2)}, u32[]{:S(2)}) collective-permute-start(bf16[32,1536]{1,0:T(8,128)(2,1)S(1)} %reshape.142), channel_id=1, source_target_pairs={{0,1},{1,0},{2,3},{3,2},{4,5},{5,4},{6,7},{7,6},{8,9},{9,8},{10,11... | collective-permute-start | bytes 294920 | tf_op jit(solution)/shard_map/ppermute | solution.py:340
  6.5 1.9 %collective-permute-start.10 = (bf16[384,1024]{1,0:T(8,128)(2,1)S(1)}, bf16[384,1024]{1,0:T(8,128)(2,1)}, u32[]{:S(2)}, u32[]{:S(2)}) collective-permute-start(bf16[384,1024]{1,0:T(8,128)(2,1)S(1)} %bitcast.258), channel_id=1, source_target_pairs={{0,1},{1,0},{2,3},{3,2},{4,5},{5,4},{6,7},{7,6},{8,9},{9,8},{10,11... | collective-permute-start | bytes 2359304 | tf_op jit(solution)/shard_map/ppermute | solution.py:340
  10.0 3.2 %collective-permute-start.2 = (bf16[2,32,1024]{2,1,0:T(8,128)(2,1)S(1)}, bf16[2,32,1024]{2,1,0:T(8,128)(2,1)S(1)}, u32[]{:S(2)}, u32[]{:S(2)}) collective-permute-start(bf16[2,32,1024]{2,1,0:T(8,128)(2,1)S(1)} %get-tuple-element.59), channel_id=1, source_target_pairs={{0,4},{2,6},{4,0},{6,2},{1,5},{3,7},{5,1},{7,3},{8,12},{10,14},{12... | collective-permute-start | bytes 393224 | tf_op jit(solution)/shard_map/ppermute | solution.py:345
  13.3 8.5 %collective-permute-done.2 = bf16[2,32,1024]{2,1,0:T(8,128)(2,1)S(1)} collective-permute-done((bf16[2,32,1024]{2,1,0:T(8,128)(2,1)S(1)}, bf16[2,32,1024]{2,1,0:T(8,128)(2,1)S(1)}, u32[]{:S(2)}, u32[]{:S(2)}) %collective-permute-start.2) | collective-permute-done | bytes 131104 | tf_op jit(solution)/shard_map/ppermute | solution.py:345
  24.7 6.5 %collective-permute-done.3 = bf16[2,2,32,1024]{3,2,1,0:T(8,128)(2,1)S(1)} collective-permute-done((bf16[2,2,32,1024]{3,2,1,0:T(8,128)(2,1)S(1)}, bf16[2,2,32,1024]{3,2,1,0:T(8,128)(2,1)S(1)}, u32[]{:S(2)}, u32[]{:S(2)}) %collective-permute-start.3) | collective-permute-done | bytes 262176 | tf_op jit(solution)/shard_map/ppermute | solution.py:345
  37.0 8.7 %collective-permute-done.4 = bf16[2,2,2,32,1024]{4,3,2,1,0:T(8,128)(2,1)} collective-permute-done((bf16[2,2,2,32,1024]{4,3,2,1,0:T(8,128)(2,1)S(1)}, bf16[2,2,2,32,1024]{4,3,2,1,0:T(8,128)(2,1)}, u32[]{:S(2)}, u32[]{:S(2)}) %collective-permute-start.4) | collective-permute-done | bytes 524320 | tf_op jit(solution)/shard_map/ppermute | solution.py:345
  47.0 1.6 select_bitcast_fusion.5
  50.0 2.2 %collective-permute-done.8 = bf16[2,2,2,32,1024]{4,3,2,1,0:T(8,128)(2,1)S(1)} collective-permute-done((bf16[2,2,2,32,1024]{4,3,2,1,0:T(8,128)(2,1)S(1)}, bf16[2,2,2,32,1024]{4,3,2,1,0:T(8,128)(2,1)S(1)}, u32[]{:S(2)}, u32[]{:S(2)}) %collective-permute-start.8) | collective-permute-done | bytes 524320 | tf_op jit(solution)/shard_map/ppermute | solution.py:345
  54.3 1.9 %convolution_convert_fusion.3.q_ref = bf16[768,512]{1,0:T(8,128)(2,1)} fusion(bf16[768,1024]{1,0:T(8,128)(2,1)S(1)} %bitcast.271, bf16[1024,1024]{1,0:T(8,128)(2,1)S(1)} %bitcast.264), kind=kOutput, calls=%fused_computation.28 | convolution fusion | flops 805699584 | bytes 3407872 | tf_op jit(solution)/shard_map/dot_general | solution.py:398
  57.7 1.7 %reshape.169 = bf16[512,1024,1]{1,0,2:T(8,128)(2,1)} reshape(bf16[2,2,2,2,32,2,512]{6,5,4,3,2,1,0:T(2,128)(2,1)S(1)} %copy.63) | data formatting | bytes 2097152 | tf_op jit(solution)/shard_map/reshape | solution.py:394
  62.4 1.9 %convolution_convert_fusion.g_ref = bf16[768,512]{1,0:T(8,128)(2,1)} fusion(bf16[768,1024]{1,0:T(8,128)(2,1)S(1)} %bitcast.275, bf16[512,1024]{1,0:T(8,128)(2,1)S(1)} %bitcast.277), kind=kOutput, calls=%fused_computation.25 | convolution fusion | flops 805699584 | bytes 3407872 | tf_op jit(solution)/shard_map/dot_general | solution.py:16
  64.3 27.4 %attention.1 = (bf16[768,512]{1,0:T(8,128)(2,1)S(1)}, bf16[768,512]{1,0:T(8,128)(2,1)S(1)}, bf16[768,512]{1,0:T(8,128)(2,1)S(1)}, bf16[768,512]{1,0:T(8,128)(2,1)S(1)}) custom-call(f32[8,6,768]{2,1,0:T(8,128)S(1)} %copy-done.1, s32[1,768]{1,0:T(1,128)S(1)} %broadcast_in_dim.23.seg_row_ref, s32[768,1]{1,0:T(8,128)S(1)} %broadcast_in_dim.27.seg_col_ref, ...), custom_call_target="tpu_custom_call" | custom-call | tf_op jit(solution)/shard_map/attention/pallas_call | solution.py:301
  92.7 2.0 %multiply_convert_fusion.1 = bf16[512,1024]{1,0:T(8,128)(2,1)} fusion(bf16[768,512]{1,0:T(8,128)(2,1)S(1)} %get-tuple-element.14, bf16[768,1024]{1,0:T(8,128)(2,1)S(1)} %bitcast.276), kind=kOutput, calls=%fused_computation.12 | convolution fusion | flops 806354944 | bytes 3407872 | tf_op jit(solution)/shard_map/dot_general | solution.py:22
  94.7 2.8 %reshape.152 = bf16[2,2,2,2,32,2,512]{6,5,4,3,2,1,0:T(2,128)(2,1)} reshape(bf16[512,1024]{1,0:T(8,128)(2,1)} %multiply_convert_fusion.1) | data formatting | bytes 2097152 | tf_op jit(solution)/shard_map/reshape | solution.py:436
  101.2 1.9 %multiply_convert_fusion = bf16[1024,1024]{1,0:T(8,128)(2,1)S(1)} fusion(bf16[768,1024]{1,0:T(8,128)(2,1)S(1)} %bitcast.274, bf16[768,1024]{1,0:T(8,128)(2,1)S(1)} %constant_dynamic-update-slice_fusion.3), kind=kOutput, calls=%fused_computation | convolution fusion | flops 1612709888 | bytes 5242880 | tf_op jit(solution)/shard_map/dot_general | solution.py:22
  106.5 1.8 %fusion.33 = f32[768,1024]{1,0:T(8,128)S(1)} fusion(bf16[768,1024]{1,0:T(8,128)(2,1)S(1)} %constant_dynamic-update-slice_fusion.3, bf16[1024,1024]{1,0:T(8,128)(2,1)S(1)} %bitcast.265), kind=kOutput, calls=%fused_computation.146 | convolution fusion | flops 1610612736 | bytes 6815744 | tf_op jit(solution)/shard_map/dot_general | solution.py:16
  113.6 10.1 %collective-permute-done.21 = bf16[2,2,2,32,1024]{4,3,2,1,0:T(8,128)(2,1)S(1)} collective-permute-done((bf16[2,2,2,32,1024]{4,3,2,1,0:T(8,128)(2,1)S(1)}, bf16[2,2,2,32,1024]{4,3,2,1,0:T(8,128)(2,1)S(1)}, u32[]{:S(2)}, u32[]{:S(2)}) %collective-permute-start.21) | collective-permute-done | bytes 524320 | tf_op jit(solution)/shard_map/ppermute | solution.py:345
  124.2 9.5 %collective-permute-done.12 = bf16[2,2,2,32,1024]{4,3,2,0,1:T(8,128)(2,1)S(1)} collective-permute-done((bf16[2,2,2,32,1024]{4,3,2,0,1:T(8,128)(2,1)S(1)}, bf16[2,2,2,32,1024]{4,3,2,0,1:T(8,128)(2,1)S(1)}, u32[]{:S(2)}, u32[]{:S(2)}) %collective-permute-start.12) | collective-permute-done | bytes 524320 | tf_op jit(solution)/shard_map/ppermute | solution.py:345
  135.6 4.8 %collective-permute-start.23 = (bf16[2,32,1024]{2,1,0:T(8,128)(2,1)S(1)}, bf16[2,32,1024]{2,1,0:T(8,128)(2,1)S(1)}, u32[]{:S(2)}, u32[]{:S(2)}) collective-permute-start(bf16[2,32,1024]{2,1,0:T(8,128)(2,1)S(1)} %dynamic-slice_bitcast_fusion.5), channel_id=1, source_target_pairs={{0,4},{2,6},{4,0},{6,2},{1,5},{3,7},{5,1},{7,3},{8,12},{10,14},{12... | collective-permute-start | bytes 393224 | tf_op jit(solution)/shard_map/ppermute | solution.py:345
  140.4 2.7 %collective-permute-done.14 = bf16[2,2,32,1024]{3,2,1,0:T(8,128)(2,1)S(1)} collective-permute-done((bf16[2,2,32,1024]{3,2,1,0:T(8,128)(2,1)S(1)}, bf16[2,2,32,1024]{3,2,1,0:T(8,128)(2,1)S(1)}, u32[]{:S(2)}, u32[]{:S(2)}) %collective-permute-start.14) | collective-permute-done | bytes 262176 | tf_op jit(solution)/shard_map/ppermute | solution.py:345
  143.2 3.1 %collective-permute-start.16 = (bf16[2,32,1024]{2,1,0:T(8,128)(2,1)S(1)}, bf16[2,32,1024]{2,1,0:T(8,128)(2,1)S(1)}, u32[]{:S(2)}, u32[]{:S(2)}) collective-permute-start(bf16[2,32,1024]{2,1,0:T(8,128)(2,1)S(1)} %dynamic-slice_bitcast_fusion.6), channel_id=1, source_target_pairs={{0,4},{2,6},{4,0},{6,2},{1,5},{3,7},{5,1},{7,3},{8,12},{10,14},{12... | collective-permute-start | bytes 393224 | tf_op jit(solution)/shard_map/ppermute | solution.py:345
  148.7 3.0 %collective-permute-done.16 = bf16[2,32,1024]{2,1,0:T(8,128)(2,1)S(1)} collective-permute-done((bf16[2,32,1024]{2,1,0:T(8,128)(2,1)S(1)}, bf16[2,32,1024]{2,1,0:T(8,128)(2,1)S(1)}, u32[]{:S(2)}, u32[]{:S(2)}) %collective-permute-start.16) | collective-permute-done | bytes 131104 | tf_op jit(solution)/shard_map/ppermute | solution.py:345
  154.4 1.7 %collective-permute-done.17 = bf16[32,1024]{1,0:T(8,128)(2,1)S(1)} collective-permute-done((bf16[32,1024]{1,0:T(8,128)(2,1)S(1)}, bf16[32,1024]{1,0:T(8,128)(2,1)S(1)}, u32[]{:S(2)}, u32[]{:S(2)}) %collective-permute-start.17) | collective-permute-done | bytes 65568 | tf_op jit(solution)/shard_map/ppermute | solution.py:340
  158.7 2.4 %collective-permute-done.18 = bf16[2,32,1024]{2,1,0:T(8,128)(2,1)S(1)} collective-permute-done((bf16[2,32,1024]{2,1,0:T(8,128)(2,1)S(1)}, bf16[2,32,1024]{2,1,0:T(8,128)(2,1)S(1)}, u32[]{:S(2)}, u32[]{:S(2)}) %collective-permute-start.18) | collective-permute-done | bytes 131104 | tf_op jit(solution)/shard_map/ppermute | solution.py:345
  (183 shorter events, 52.7 us)
Async XLA Ops:
  3.4 6.5 %collective-permute-start.1 = (bf16[32,1536]{1,0:T(8,128)(2,1)S(1)}, bf16[32,1536]{1,0:T(8,128)(2,1)S(1)}, u32[]{:S(2)}, u32[]{:S(2)}) collective-permute-start(bf16[32,1536]{1,0:T(8,128)(2,1)S(1)} %reshape.142), channel_id=1, source_target_pairs={{0,1},{1,0},{2,3},{3,2},{4,5},{5,4},{6,7},{7,6},{8,9},{9,8},{10,11... | collective-permute-start | bytes 294920 | tf_op jit(solution)/shard_map/ppermute | solution.py:340
  6.4 40.5 %collective-permute-start = (bf16[384,1024]{1,0:T(8,128)(2,1)S(1)}, bf16[384,1024]{1,0:T(8,128)(2,1)}, u32[]{:S(2)}, u32[]{:S(2)}) collective-permute-start(bf16[384,1024]{1,0:T(8,128)(2,1)S(1)} %bitcast.257), channel_id=1, source_target_pairs={{0,1},{1,0},{2,3},{3,2},{4,5},{5,4},{6,7},{7,6},{8,9},{9,8},{10,11... | collective-permute-start | bytes 2359304 | tf_op jit(solution)/shard_map/ppermute | solution.py:340
  6.5 40.5 %collective-permute-start.10 = (bf16[384,1024]{1,0:T(8,128)(2,1)S(1)}, bf16[384,1024]{1,0:T(8,128)(2,1)}, u32[]{:S(2)}, u32[]{:S(2)}) collective-permute-start(bf16[384,1024]{1,0:T(8,128)(2,1)S(1)} %bitcast.258), channel_id=1, source_target_pairs={{0,1},{1,0},{2,3},{3,2},{4,5},{5,4},{6,7},{7,6},{8,9},{9,8},{10,11... | collective-permute-start | bytes 2359304 | tf_op jit(solution)/shard_map/ppermute | solution.py:340
  10.0 11.9 %collective-permute-start.2 = (bf16[2,32,1024]{2,1,0:T(8,128)(2,1)S(1)}, bf16[2,32,1024]{2,1,0:T(8,128)(2,1)S(1)}, u32[]{:S(2)}, u32[]{:S(2)}) collective-permute-start(bf16[2,32,1024]{2,1,0:T(8,128)(2,1)S(1)} %get-tuple-element.59), channel_id=1, source_target_pairs={{0,4},{2,6},{4,0},{6,2},{1,5},{3,7},{5,1},{7,3},{8,12},{10,14},{12... | collective-permute-start | bytes 393224 | tf_op jit(solution)/shard_map/ppermute | solution.py:345
  13.2 10.3 %collective-permute-start.6 = (bf16[2,32,1024]{2,1,0:T(8,128)(2,1)S(1)}, bf16[2,32,1024]{2,1,0:T(8,128)(2,1)S(1)}, u32[]{:S(2)}, u32[]{:S(2)}) collective-permute-start(bf16[2,32,1024]{2,1,0:T(8,128)(2,1)S(1)} %get-tuple-element.58), channel_id=1, source_target_pairs={{0,4},{2,6},{4,0},{6,2},{1,5},{3,7},{5,1},{7,3},{8,12},{10,14},{12... | collective-permute-start | bytes 393224 | tf_op jit(solution)/shard_map/ppermute | solution.py:345
  21.9 9.3 %collective-permute-start.3 = (bf16[2,2,32,1024]{3,2,1,0:T(8,128)(2,1)S(1)}, bf16[2,2,32,1024]{3,2,1,0:T(8,128)(2,1)S(1)}, u32[]{:S(2)}, u32[]{:S(2)}) collective-permute-start(bf16[2,2,32,1024]{3,2,1,0:T(8,128)(2,1)S(1)} %pad_maximum_fusion.8), channel_id=1, source_target_pairs={{0,2},{2,0},{4,6},{6,4},{1,3},{3,1},{5,7},{7,5},{8,10},{10,8},{12,... | collective-permute-start | bytes 786440 | tf_op jit(solution)/shard_map/ppermute | solution.py:345
  24.2 10.5 %collective-permute-start.7 = (bf16[2,2,32,1024]{3,2,1,0:T(8,128)(2,1)}, bf16[2,2,32,1024]{3,2,1,0:T(8,128)(2,1)}, u32[]{:S(2)}, u32[]{:S(2)}) collective-permute-start(bf16[2,2,32,1024]{3,2,1,0:T(8,128)(2,1)} %pad_maximum_fusion.9), channel_id=1, source_target_pairs={{0,2},{2,0},{4,6},{6,4},{1,3},{3,1},{5,7},{7,5},{8,10},{10,8},{12,... | collective-permute-start | bytes 786440 | tf_op jit(solution)/shard_map/ppermute | solution.py:345
  31.3 14.4 %collective-permute-start.4 = (bf16[2,2,2,32,1024]{4,3,2,1,0:T(8,128)(2,1)S(1)}, bf16[2,2,2,32,1024]{4,3,2,1,0:T(8,128)(2,1)}, u32[]{:S(2)}, u32[]{:S(2)}) collective-permute-start(bf16[2,2,2,32,1024]{4,3,2,1,0:T(8,128)(2,1)S(1)} %pad_maximum_fusion.5), channel_id=1, source_target_pairs={{0,16},{8,24},{16,0},{24,8},{1,17},{9,25},{17,1},{25,9},{2,18},{10... | collective-permute-start | bytes 1572872 | tf_op jit(solution)/shard_map/ppermute | solution.py:345
  35.7 16.4 %collective-permute-start.8 = (bf16[2,2,2,32,1024]{4,3,2,1,0:T(8,128)(2,1)S(1)}, bf16[2,2,2,32,1024]{4,3,2,1,0:T(8,128)(2,1)S(1)}, u32[]{:S(2)}, u32[]{:S(2)}) collective-permute-start(bf16[2,2,2,32,1024]{4,3,2,1,0:T(8,128)(2,1)S(1)} %pad_maximum_fusion.6), channel_id=1, source_target_pairs={{0,16},{8,24},{16,0},{24,8},{1,17},{9,25},{17,1},{25,9},{2,18},{10... | collective-permute-start | bytes 1572872 | tf_op jit(solution)/shard_map/ppermute | solution.py:345
  46.9 5.5 %collective-permute-start.5 = (bf16[2,2,2,2,32,1024]{5,4,3,2,1,0:T(8,128)(2,1)S(1)}, bf16[2,2,2,2,32,1024]{5,4,3,2,1,0:T(8,128)(2,1)S(1)}, u32[]{:S(2)}, u32[]{:S(2)}) collective-permute-start(bf16[2,2,2,2,32,1024]{5,4,3,2,1,0:T(8,128)(2,1)S(1)} %pad_maximum_fusion.3), channel_id=1, source_target_pairs={{0,8},{8,0},{16,24},{24,16},{1,9},{9,1},{17,25},{25,17},{2,10},{10... | collective-permute-start | bytes 3145736 | tf_op jit(solution)/shard_map/ppermute | solution.py:345
  100.4 8.0 %collective-permute-start.20 = (bf16[2,2,2,2,32,1024]{5,4,3,2,1,0:T(8,128)(2,1)S(1)}, bf16[2,2,2,2,32,1024]{5,4,3,2,1,0:T(8,128)(2,1)S(1)}, u32[]{:S(2)}, u32[]{:S(2)}) collective-permute-start(bf16[2,2,2,2,32,1024]{5,4,3,2,1,0:T(8,128)(2,1)S(1)} %fusion.9), channel_id=1, source_target_pairs={{0,8},{8,0},{16,24},{24,16},{1,9},{9,1},{17,25},{25,17},{2,10},{10... | collective-permute-start | bytes 3145736 | tf_op jit(solution)/shard_map/ppermute | solution.py:345
  103.1 7.2 %collective-permute-start.11 = (bf16[2,2,2,2,32,1024]{5,4,0,3,1,2:T(8,128)(2,1)S(1)}, bf16[2,2,2,2,32,1024]{5,4,0,3,1,2:T(8,128)(2,1)S(1)}, u32[]{:S(2)}, u32[]{:S(2)}) collective-permute-start(bf16[2,2,2,2,32,1024]{5,4,0,3,1,2:T(8,128)(2,1)S(1)} %dynamic-slice_bitcast_fusion), channel_id=1, source_target_pairs={{0,8},{8,0},{16,24},{24,16},{1,9},{9,1},{17,25},{25,17},{2,10},{10... | collective-permute-start | bytes 3145736 | tf_op jit(solution)/shard_map/ppermute | solution.py:345
  105.4 28.5 %collective-permute-start.13 = (bf16[384,1024]{1,0:T(8,128)(2,1)S(1)}, bf16[384,1024]{1,0:T(8,128)(2,1)S(1)}, u32[]{:S(2)}, u32[]{:S(2)}) collective-permute-start(bf16[384,1024]{1,0:T(8,128)(2,1)S(1)} %fusion.17), channel_id=1, source_target_pairs={{0,1},{1,0},{2,3},{3,2},{4,5},{5,4},{6,7},{7,6},{8,9},{9,8},{10,11... | collective-permute-start | bytes 2359304 | tf_op jit(solution)/shard_map/ppermute | solution.py:340
  108.8 14.9 %collective-permute-start.21 = (bf16[2,2,2,32,1024]{4,3,2,1,0:T(8,128)(2,1)S(1)}, bf16[2,2,2,32,1024]{4,3,2,1,0:T(8,128)(2,1)S(1)}, u32[]{:S(2)}, u32[]{:S(2)}) collective-permute-start(bf16[2,2,2,32,1024]{4,3,2,1,0:T(8,128)(2,1)S(1)} %dynamic-slice_bitcast_fusion.1), channel_id=1, source_target_pairs={{0,16},{8,24},{16,0},{24,8},{1,17},{9,25},{17,1},{25,9},{2,18},{10... | collective-permute-start | bytes 1572872 | tf_op jit(solution)/shard_map/ppermute | solution.py:345
  110.9 22.8 %collective-permute-start.12 = (bf16[2,2,2,32,1024]{4,3,2,0,1:T(8,128)(2,1)S(1)}, bf16[2,2,2,32,1024]{4,3,2,0,1:T(8,128)(2,1)S(1)}, u32[]{:S(2)}, u32[]{:S(2)}) collective-permute-start(bf16[2,2,2,32,1024]{4,3,2,0,1:T(8,128)(2,1)S(1)} %dynamic-slice_bitcast_fusion.2), channel_id=1, source_target_pairs={{0,16},{8,24},{16,0},{24,8},{1,17},{9,25},{17,1},{25,9},{2,18},{10... | collective-permute-start | bytes 1572872 | tf_op jit(solution)/shard_map/ppermute | solution.py:345
  112.6 30.6 %collective-permute-start.15 = (bf16[384,1024]{1,0:T(8,128)(2,1)S(1)}, bf16[384,1024]{1,0:T(8,128)(2,1)S(1)}, u32[]{:S(2)}, u32[]{:S(2)}) collective-permute-start(bf16[384,1024]{1,0:T(8,128)(2,1)S(1)} %fusion.18), channel_id=1, source_target_pairs={{0,1},{1,0},{2,3},{3,2},{4,5},{5,4},{6,7},{7,6},{8,9},{9,8},{10,11... | collective-permute-start | bytes 2359304 | tf_op jit(solution)/shard_map/ppermute | solution.py:340
  124.0 11.5 %collective-permute-start.22 = (bf16[2,2,32,1024]{3,2,1,0:T(8,128)(2,1)S(1)}, bf16[2,2,32,1024]{3,2,1,0:T(8,128)(2,1)S(1)}, u32[]{:S(2)}, u32[]{:S(2)}) collective-permute-start(bf16[2,2,32,1024]{3,2,1,0:T(8,128)(2,1)S(1)} %dynamic-slice_bitcast_fusion.3), channel_id=1, source_target_pairs={{0,2},{2,0},{4,6},{6,4},{1,3},{3,1},{5,7},{7,5},{8,10},{10,8},{12,... | collective-permute-start | bytes 786440 | tf_op jit(solution)/shard_map/ppermute | solution.py:345
  134.0 9.1 %collective-permute-start.14 = (bf16[2,2,32,1024]{3,2,1,0:T(8,128)(2,1)S(1)}, bf16[2,2,32,1024]{3,2,1,0:T(8,128)(2,1)S(1)}, u32[]{:S(2)}, u32[]{:S(2)}) collective-permute-start(bf16[2,2,32,1024]{3,2,1,0:T(8,128)(2,1)S(1)} %dynamic-slice_bitcast_fusion.4), channel_id=1, source_target_pairs={{0,2},{2,0},{4,6},{6,4},{1,3},{3,1},{5,7},{7,5},{8,10},{10,8},{12,... | collective-permute-start | bytes 786440 | tf_op jit(solution)/shard_map/ppermute | solution.py:345
  135.6 12.0 %collective-permute-start.23 = (bf16[2,32,1024]{2,1,0:T(8,128)(2,1)S(1)}, bf16[2,32,1024]{2,1,0:T(8,128)(2,1)S(1)}, u32[]{:S(2)}, u32[]{:S(2)}) collective-permute-start(bf16[2,32,1024]{2,1,0:T(8,128)(2,1)S(1)} %dynamic-slice_bitcast_fusion.5), channel_id=1, source_target_pairs={{0,4},{2,6},{4,0},{6,2},{1,5},{3,7},{5,1},{7,3},{8,12},{10,14},{12... | collective-permute-start | bytes 393224 | tf_op jit(solution)/shard_map/ppermute | solution.py:345
  143.2 8.5 %collective-permute-start.16 = (bf16[2,32,1024]{2,1,0:T(8,128)(2,1)S(1)}, bf16[2,32,1024]{2,1,0:T(8,128)(2,1)S(1)}, u32[]{:S(2)}, u32[]{:S(2)}) collective-permute-start(bf16[2,32,1024]{2,1,0:T(8,128)(2,1)S(1)} %dynamic-slice_bitcast_fusion.6), channel_id=1, source_target_pairs={{0,4},{2,6},{4,0},{6,2},{1,5},{3,7},{5,1},{7,3},{8,12},{10,14},{12... | collective-permute-start | bytes 393224 | tf_op jit(solution)/shard_map/ppermute | solution.py:345
  147.6 5.1 %collective-permute-start.24 = (bf16[32,512]{1,0:T(8,128)(2,1)S(1)}, bf16[32,512]{1,0:T(8,128)(2,1)S(1)}, u32[]{:S(2)}, u32[]{:S(2)}) collective-permute-start(bf16[32,512]{1,0:T(8,128)(2,1)S(1)} %dynamic-slice_bitcast_fusion.8), channel_id=1, source_target_pairs={{0,1},{1,0},{2,3},{3,2},{4,5},{5,4},{6,7},{7,6},{8,9},{9,8},{10,11... | collective-permute-start | bytes 98312 | tf_op jit(solution)/shard_map/ppermute | solution.py:340
  151.7 4.3 %collective-permute-start.17 = (bf16[32,1024]{1,0:T(8,128)(2,1)S(1)}, bf16[32,1024]{1,0:T(8,128)(2,1)S(1)}, u32[]{:S(2)}, u32[]{:S(2)}) collective-permute-start(bf16[32,1024]{1,0:T(8,128)(2,1)S(1)} %dynamic-slice_bitcast_fusion.7), channel_id=1, source_target_pairs={{0,1},{1,0},{2,3},{3,2},{4,5},{5,4},{6,7},{7,6},{8,9},{9,8},{10,11... | collective-permute-start | bytes 196616 | tf_op jit(solution)/shard_map/ppermute | solution.py:340
  152.8 5.7 %collective-permute-start.25 = (bf16[2,32,1024]{2,1,0:T(8,128)(2,1)S(1)}, bf16[2,32,1024]{2,1,0:T(8,128)(2,1)S(1)}, u32[]{:S(2)}, u32[]{:S(2)}) collective-permute-start(bf16[2,32,1024]{2,1,0:T(8,128)(2,1)S(1)} %pad_maximum_fusion.14), channel_id=1, source_target_pairs={{0,16},{8,24},{16,0},{24,8},{1,17},{9,25},{17,1},{25,9},{2,18},{10... | collective-permute-start | bytes 393224 | tf_op jit(solution)/shard_map/ppermute | solution.py:345
  156.1 5.0 %collective-permute-start.18 = (bf16[2,32,1024]{2,1,0:T(8,128)(2,1)S(1)}, bf16[2,32,1024]{2,1,0:T(8,128)(2,1)S(1)}, u32[]{:S(2)}, u32[]{:S(2)}) collective-permute-start(bf16[2,32,1024]{2,1,0:T(8,128)(2,1)S(1)} %pad_maximum_fusion.13), channel_id=1, source_target_pairs={{0,16},{8,24},{16,0},{24,8},{1,17},{9,25},{17,1},{25,9},{2,18},{10... | collective-permute-start | bytes 393224 | tf_op jit(solution)/shard_map/ppermute | solution.py:345
  (22 other events, 110.6 us)
